TPU v7x, 32 devices: a whole 2x2x4 slice. The times are simulated.
32 devices in a mesh: wide: 16 (over z, y, x), tp: 2 (over core).
Axes of the slice: x: 2, y: 2, z: 4, core: 2. Of those that a mesh axis runs over, the one named last changes fastest.
Arguments:
- tokens: bfloat16 [32, 256, 1152], P('wide', 'tp'), may hold values from -6 to 6
- cotangent: bfloat16 [32, 256, 1152], P('wide', 'tp'), may hold values from -6 to 6
- caption: bfloat16 [240, 4096], P('wide'), may hold values from -6 to 6
- caption_len: int32 [2], replicated, may hold values from 5 to 120, as said below
- clip_id: int32 [32], replicated, may hold values from 0 to 1, never falling along the last dimension, each value on 1 to 31 neighbouring positions
- timestep: int32 [2], replicated, may hold values from 0 to 999
- w_mod: bfloat16 [1152, 6912], P(None, 'tp'), may hold values from -0.1875 to 0.1875
- b_mod: bfloat16 [6912], P('tp'), may hold values from 0.5 to 1.5
- w_text: bfloat16 [4096, 1152], P(None, 'tp'), may hold values from -0.09375 to 0.09375
- w_sqkv: bfloat16 [1152, 3, 1152], P(None, None, 'tp'), may hold values from -0.1875 to 0.1875
- w_so: bfloat16 [1152, 1152], P('tp'), may hold values from -0.75 to 0.75
- w_tqkv: bfloat16 [1152, 3, 1152], P(None, None, 'tp'), may hold values from -0.1875 to 0.1875
- w_to: bfloat16 [1152, 1152], P('tp'), may hold values from -0.375 to 0.375
- w_cq: bfloat16 [1152, 1152], P(None, 'tp'), may hold values from -0.1875 to 0.1875
- w_ckv: bfloat16 [1152, 2, 1152], P(None, None, 'tp'), may hold values from -0.1875 to 0.1875
- w_co: bfloat16 [1152, 1152], P('tp'), may hold values from -0.5 to 0.5
- w_fc1: bfloat16 [1152, 4608], P(None, 'tp'), may hold values from -0.1875 to 0.1875
- w_fc2: bfloat16 [4608, 1152], P('tp'), may hold values from -0.09375 to 0.09375
Outputs:
- block_out: bfloat16 [32, 256, 1152], P('wide', 'tp')
- grad_tokens: bfloat16 [32, 256, 1152], P('wide', 'tp')
- grad_w_mod: float32 [1152, 6912], P(None, ('tp', 'wide'))
- grad_b_mod: float32 [6912], P(('tp', 'wide'))
- grad_w_text: float32 [4096, 1152], P('wide', 'tp')
- grad_w_sqkv: float32 [1152, 3, 1152], P('wide', None, 'tp')
- grad_w_so: float32 [1152, 1152], P('tp', 'wide')
- grad_w_tqkv: float32 [1152, 3, 1152], P('wide', None, 'tp')
- grad_w_to: float32 [1152, 1152], P('tp', 'wide')
- grad_w_cq: float32 [1152, 1152], P('wide', 'tp')
- grad_w_ckv: float32 [1152, 2, 1152], P('wide', None, 'tp')
- grad_w_co: float32 [1152, 1152], P('tp', 'wide')
- grad_w_fc1: float32 [1152, 4608], P('wide', 'tp')
- grad_w_fc2: float32 [4608, 1152], P('tp', 'wide')
Inputs may be any that keep to these rules, and one draw needn't show every extreme that they name: `clip_id`: frame ids never fall; every clip has 1 to 31 frames. A clip's real caption tokens are the first caption_len rows of its 120; some clip fills all 120.
All inputs are finite; a program needn't handle non-finite values.
Results may differ from a plain program's by a relative error of at most 0.03.
Values may be sent and summed in bfloat16 or wider, within the bound.
A program may use at most 256 MiB of HBM per device.

v0:
```python
import math

import jax
import jax.numpy as jnp
from jax import lax
from jax.sharding import PartitionSpec as P

HD = 72
LTXT = 120


EPS = 1e-06
NEGATIVE = -1e30
HIGH = lax.Precision.HIGHEST


def layer_norm(operand):
    average = jnp.mean(operand, axis=-1, keepdims=True)
    centred = operand - average
    spread = jnp.mean(centred * centred, axis=-1, keepdims=True)
    inverse = lax.rsqrt(spread + EPS)
    return (centred * inverse, inverse)


def norm_back(grad_normed, normed, inverse):
    grad_mean = jnp.mean(grad_normed, axis=-1, keepdims=True)
    grad_cross = jnp.mean(grad_normed * normed, axis=-1, keepdims=True)
    return inverse * (grad_normed - grad_mean - normed * grad_cross)


def gelu_tanh(operand):
    return jax.nn.gelu(operand, approximate=True)


def masked_scores(queries, key_rows, allowed, factor):
    scores = (
        jnp.einsum("...qd,...kd->...qk", queries, key_rows, preferred_element_type=jnp.float32)
        * factor
    )
    if allowed is None:
        return scores
    return jnp.where(allowed, scores, NEGATIVE)


def attend_forward(queries, key_rows, value_rows, allowed, factor):
    scores = masked_scores(queries, key_rows, allowed, factor)
    largest = jnp.max(scores, axis=-1, keepdims=True)
    log_total = largest + jnp.log(jnp.sum(jnp.exp(scores - largest), axis=-1, keepdims=True))
    attn_probs = jnp.exp(scores - log_total).astype(jnp.bfloat16)
    output = jnp.einsum(
        "...qk,...kd->...qd", attn_probs, value_rows, preferred_element_type=jnp.float32
    )
    return (output.astype(jnp.bfloat16), log_total)


def attend_backward(queries, key_rows, value_rows, log_total, grad_out, allowed, factor):
    attn_probs = jnp.exp(masked_scores(queries, key_rows, allowed, factor) - log_total)
    grad_probs = jnp.einsum(
        "...qd,...kd->...qk", grad_out, value_rows, preferred_element_type=jnp.float32
    )
    row_dot = jnp.sum(attn_probs * grad_probs, axis=-1, keepdims=True)
    grad_scores = (attn_probs * (grad_probs - row_dot)).astype(jnp.bfloat16)
    grad_queries = (
        jnp.einsum("...qk,...kd->...qd", grad_scores, key_rows, preferred_element_type=jnp.float32)
        * factor
    )
    grad_keys = (
        jnp.einsum("...qk,...qd->...kd", grad_scores, queries, preferred_element_type=jnp.float32)
        * factor
    )
    grad_values = jnp.einsum(
        "...qk,...qd->...kd",
        attn_probs.astype(jnp.bfloat16),
        grad_out,
        preferred_element_type=jnp.float32,
    )
    return (grad_queries, grad_keys, grad_values)


def spread_rows(operand):
    return lax.all_gather(operand, "tp", axis=1, tiled=True)


def collect_rows(partial_sum):
    return lax.psum_scatter(
        partial_sum.astype(jnp.bfloat16), "tp", scatter_dimension=1, tiled=True
    ).astype(jnp.float32)


def spread_grads(operand):
    return lax.all_gather(operand, "tp", axis=1, tiled=True)


def collect_grads(partial_sum):
    return lax.psum_scatter(
        partial_sum.astype(jnp.bfloat16), "tp", scatter_dimension=1, tiled=True
    ).astype(jnp.float32)


def return_frames(operand):
    return lax.all_to_all(operand, "wide", split_axis=0, concat_axis=1, tiled=True)


def return_grads(operand):
    return lax.all_to_all(operand, "wide", split_axis=0, concat_axis=1, tiled=True)


def temporal_heads(gathered):
    return gathered.reshape(
        gathered.shape[0], gathered.shape[1], gathered.shape[2], 3, HD
    ).transpose(3, 1, 2, 0, 4)


def on_device(
    tokens,
    cotangent,
    caption,
    caption_len,
    clip_id,
    timestep,
    w_mod,
    b_mod,
    w_text,
    w_sqkv,
    w_so,
    w_tqkv,
    w_to,
    w_cq,
    w_ckv,
    w_co,
    w_fc1,
    w_fc2,
):
    frames_here, patch_part, model_width = tokens.shape
    local_cols = w_so.shape[0]
    heads_here = local_cols // HD
    patches = patch_part * lax.axis_size("tp")
    row_count = frames_here * patches
    clip_count = timestep.shape[0]
    factor = HD ** (-0.5)
    wide_at = lax.axis_index("wide")
    my_clips = lax.dynamic_slice_in_dim(clip_id, wide_at * frames_here, frames_here)
    clip_onehot = (my_clips[:, None] == jnp.arange(clip_count)[None, :]).astype(jnp.float32)
    same_clip = clip_id[:, None] == clip_id[None, :]
    half_width = model_width // 2
    frequencies = jnp.exp(
        -math.log(10000.0) * jnp.arange(half_width).astype(jnp.float32) / half_width
    )
    angles = timestep.astype(jnp.float32)[:, None] * frequencies[None, :]
    embedding = jnp.concatenate([jnp.cos(angles), jnp.sin(angles)], axis=1)
    silu_embed = jax.nn.silu(embedding).astype(jnp.bfloat16)
    mod_part = (
        jnp.dot(silu_embed, w_mod, preferred_element_type=jnp.float32) + b_mod.astype(jnp.float32)
    ).astype(jnp.bfloat16)
    context_part = jnp.dot(caption, w_text, preferred_element_type=jnp.float32).astype(jnp.bfloat16)
    modulation, context = (
        lax.all_gather(mod_part, "tp", axis=1, tiled=True),
        lax.all_gather(context_part, "tp", axis=1, tiled=True),
    )
    frame_mod = jnp.dot(clip_onehot, modulation.astype(jnp.float32), precision=HIGH)
    pieces = [
        frame_mod[:, None, slot_index * model_width : (slot_index + 1) * model_width]
        for slot_index in range(6)
    ]
    shift_one, scale_one, gate_one, shift_two, scale_two, gate_two = pieces
    keyval_part = jnp.dot(
        context, w_ckv.reshape(model_width, 2 * local_cols), preferred_element_type=jnp.float32
    ).astype(jnp.bfloat16)
    keyval_all = lax.all_gather(keyval_part, "wide", axis=0, tiled=True)
    stream = tokens.astype(jnp.float32)
    normed_one, inverse_one = layer_norm(stream)
    h_one = spread_rows((normed_one * (1.0 + scale_one) + shift_one).astype(jnp.bfloat16)).reshape(
        row_count, model_width
    )
    qkv_one = jnp.dot(
        h_one, w_sqkv.reshape(model_width, 3 * local_cols), preferred_element_type=jnp.float32
    ).astype(jnp.bfloat16)
    heads_one = qkv_one.reshape(frames_here, patches, 3, heads_here, HD).transpose(2, 0, 3, 1, 4)
    out_one, total_one = attend_forward(heads_one[0], heads_one[1], heads_one[2], None, factor)
    attn_one = out_one.transpose(0, 2, 1, 3).reshape(row_count, local_cols)
    y_one = collect_rows(
        jnp.dot(attn_one, w_so, preferred_element_type=jnp.float32).reshape(
            frames_here, patches, model_width
        )
    )
    stream_one = stream + gate_one * y_one
    normed_two, inverse_two = layer_norm(stream_one)
    h_two = spread_rows(normed_two.astype(jnp.bfloat16)).reshape(row_count, model_width)
    qkv_two = jnp.dot(
        h_two, w_tqkv.reshape(model_width, 3 * local_cols), preferred_element_type=jnp.float32
    ).astype(jnp.bfloat16)
    items_two = (
        qkv_two.reshape(frames_here, patches, 3, heads_here, HD)
        .transpose(0, 1, 3, 2, 4)
        .reshape(frames_here, patches, heads_here, 3 * HD)
    )
    split = temporal_heads(
        lax.all_to_all(items_two, "wide", split_axis=1, concat_axis=0, tiled=True)
    )
    output, unused = attend_forward(split[0], split[1], split[2], same_clip, factor)
    attn_two = return_frames(output.transpose(2, 0, 1, 3)).reshape(row_count, local_cols)
    y_two = collect_rows(
        jnp.dot(attn_two, w_to, preferred_element_type=jnp.float32).reshape(
            frames_here, patches, model_width
        )
    )
    stream_two = stream_one + y_two
    normed_three, inverse_three = layer_norm(stream_two)
    h_three = spread_rows(normed_three.astype(jnp.bfloat16)).reshape(row_count, model_width)
    query_three = jnp.dot(h_three, w_cq, preferred_element_type=jnp.float32).astype(jnp.bfloat16)
    query_three = query_three.reshape(frames_here, patches, heads_here, HD).transpose(0, 2, 1, 3)
    kv_clips = keyval_all.reshape(clip_count, LTXT, 2, heads_here, HD)
    kv_frames = jnp.take(kv_clips, my_clips, axis=0).transpose(2, 0, 3, 1, 4)
    caption_ok = (jnp.arange(LTXT)[None, :] < jnp.take(caption_len, my_clips)[:, None])[
        :, None, None, :
    ]
    out_three, total_three = attend_forward(
        query_three, kv_frames[0], kv_frames[1], caption_ok, factor
    )
    attn_three = out_three.transpose(0, 2, 1, 3).reshape(row_count, local_cols)
    y_three = collect_rows(
        jnp.dot(attn_three, w_co, preferred_element_type=jnp.float32).reshape(
            frames_here, patches, model_width
        )
    )
    stream_three = stream_two + y_three
    normed_four, inverse_four = layer_norm(stream_three)
    h_four = spread_rows(
        (normed_four * (1.0 + scale_two) + shift_two).astype(jnp.bfloat16)
    ).reshape(row_count, model_width)
    upper = jnp.dot(h_four, w_fc1, preferred_element_type=jnp.float32)
    active = gelu_tanh(upper).astype(jnp.bfloat16)
    y_four = collect_rows(
        jnp.dot(active, w_fc2, preferred_element_type=jnp.float32).reshape(
            frames_here, patches, model_width
        )
    )
    block_out = (stream_three + gate_two * y_four).astype(jnp.bfloat16)
    grad_stream = cotangent.astype(jnp.float32)
    grad_gate_two = jnp.sum(grad_stream * y_four, axis=1)
    grad_y4 = spread_grads((gate_two * grad_stream).astype(jnp.bfloat16)).reshape(
        row_count, model_width
    )
    grad_fc2 = jnp.dot(active.T, grad_y4, preferred_element_type=jnp.float32)
    grad_active = jnp.dot(grad_y4, w_fc2.T, preferred_element_type=jnp.float32)
    unused, gelu_back = jax.vjp(gelu_tanh, upper)
    grad_upper = gelu_back(grad_active)[0].astype(jnp.bfloat16)
    grad_fc1 = jnp.dot(h_four.T, grad_upper, preferred_element_type=jnp.float32)
    grad_h4 = collect_grads(
        jnp.dot(grad_upper, w_fc1.T, preferred_element_type=jnp.float32).reshape(
            frames_here, patches, model_width
        )
    )
    grad_shift_two = jnp.sum(grad_h4, axis=1)
    grad_scale_two = jnp.sum(grad_h4 * normed_four, axis=1)
    grad_stream = grad_stream + norm_back(grad_h4 * (1.0 + scale_two), normed_four, inverse_four)
    grad_y3 = spread_grads(grad_stream.astype(jnp.bfloat16)).reshape(row_count, model_width)
    grad_co = jnp.dot(attn_three.T, grad_y3, preferred_element_type=jnp.float32)
    grad_attn3 = jnp.dot(grad_y3, w_co.T, preferred_element_type=jnp.float32).astype(jnp.bfloat16)
    grad_attn3 = grad_attn3.reshape(frames_here, patches, heads_here, HD).transpose(0, 2, 1, 3)
    grads_three = attend_backward(
        query_three, kv_frames[0], kv_frames[1], total_three, grad_attn3, caption_ok, factor
    )
    grad_q3 = (
        grads_three[0].astype(jnp.bfloat16).transpose(0, 2, 1, 3).reshape(row_count, local_cols)
    )
    grad_cq = jnp.dot(h_three.T, grad_q3, preferred_element_type=jnp.float32)
    grad_h3 = collect_grads(
        jnp.dot(grad_q3, w_cq.T, preferred_element_type=jnp.float32).reshape(
            frames_here, patches, model_width
        )
    )
    grad_kv_frames = (
        jnp.stack([grads_three[1], grads_three[2]], axis=0)
        .transpose(1, 3, 0, 2, 4)
        .reshape(frames_here, LTXT * 2 * local_cols)
    )
    grad_kv_clips = jnp.dot(clip_onehot.T, grad_kv_frames, precision=HIGH).reshape(
        clip_count * LTXT, 2 * local_cols
    )
    grad_kv = lax.psum_scatter(grad_kv_clips, "wide", scatter_dimension=0, tiled=True).astype(
        jnp.bfloat16
    )
    grad_ckv = jnp.dot(context.T, grad_kv, preferred_element_type=jnp.float32).reshape(
        model_width, 2, local_cols
    )
    grad_context_part = jnp.dot(
        grad_kv, w_ckv.reshape(model_width, 2 * local_cols).T, preferred_element_type=jnp.float32
    )
    grad_stream = grad_stream + norm_back(grad_h3, normed_three, inverse_three)
    grad_y2 = spread_grads(grad_stream.astype(jnp.bfloat16)).reshape(row_count, model_width)
    grad_to = jnp.dot(attn_two.T, grad_y2, preferred_element_type=jnp.float32)
    grad_attn2 = jnp.dot(grad_y2, w_to.T, preferred_element_type=jnp.float32).astype(jnp.bfloat16)
    grad_attn2 = grad_attn2.reshape(frames_here, patches, heads_here, HD)
    grad_patch = lax.all_to_all(grad_attn2, "wide", split_axis=1, concat_axis=0, tiled=True)
    gathered = lax.all_to_all(items_two, "wide", split_axis=1, concat_axis=0, tiled=True)
    split = temporal_heads(gathered)
    unused_out, log_total = attend_forward(split[0], split[1], split[2], same_clip, factor)
    grads = attend_backward(
        split[0], split[1], split[2], log_total, grad_patch.transpose(1, 2, 0, 3), same_clip, factor
    )
    stacked = jnp.stack(grads, axis=3).astype(jnp.bfloat16)
    grad_items = return_grads(stacked.transpose(2, 0, 1, 3, 4).reshape(gathered.shape))
    grad_qkv2 = (
        grad_items.reshape(frames_here, patches, heads_here, 3, HD)
        .transpose(0, 1, 3, 2, 4)
        .reshape(row_count, 3 * local_cols)
    )
    grad_tqkv = jnp.dot(h_two.T, grad_qkv2, preferred_element_type=jnp.float32).reshape(
        model_width, 3, local_cols
    )
    grad_h2 = collect_grads(
        jnp.dot(
            grad_qkv2,
            w_tqkv.reshape(model_width, 3 * local_cols).T,
            preferred_element_type=jnp.float32,
        ).reshape(frames_here, patches, model_width)
    )
    grad_stream = grad_stream + norm_back(grad_h2, normed_two, inverse_two)
    grad_gate_one = jnp.sum(grad_stream * y_one, axis=1)
    grad_y1 = spread_grads((gate_one * grad_stream).astype(jnp.bfloat16)).reshape(
        row_count, model_width
    )
    grad_so = jnp.dot(attn_one.T, grad_y1, preferred_element_type=jnp.float32)
    grad_attn1 = jnp.dot(grad_y1, w_so.T, preferred_element_type=jnp.float32).astype(jnp.bfloat16)
    grad_attn1 = grad_attn1.reshape(frames_here, patches, heads_here, HD).transpose(0, 2, 1, 3)
    grads_one = attend_backward(
        heads_one[0], heads_one[1], heads_one[2], total_one, grad_attn1, None, factor
    )
    grad_qkv1 = (
        jnp.stack(grads_one, axis=0)
        .astype(jnp.bfloat16)
        .transpose(1, 3, 0, 2, 4)
        .reshape(row_count, 3 * local_cols)
    )
    grad_sqkv = jnp.dot(h_one.T, grad_qkv1, preferred_element_type=jnp.float32).reshape(
        model_width, 3, local_cols
    )
    grad_h1 = collect_grads(
        jnp.dot(
            grad_qkv1,
            w_sqkv.reshape(model_width, 3 * local_cols).T,
            preferred_element_type=jnp.float32,
        ).reshape(frames_here, patches, model_width)
    )
    grad_shift_one = jnp.sum(grad_h1, axis=1)
    grad_scale_one = jnp.sum(grad_h1 * normed_one, axis=1)
    grad_stream = grad_stream + norm_back(grad_h1 * (1.0 + scale_one), normed_one, inverse_one)
    grad_tokens = grad_stream.astype(jnp.bfloat16)
    grad_frame_mod = jnp.concatenate(
        [
            grad_shift_one,
            grad_scale_one,
            grad_gate_one,
            grad_shift_two,
            grad_scale_two,
            grad_gate_two,
        ],
        axis=1,
    )
    grad_mod_full = jnp.dot(clip_onehot.T, grad_frame_mod, precision=HIGH)
    grad_context, grad_mod = (
        lax.psum_scatter(
            grad_context_part.astype(jnp.bfloat16), "tp", scatter_dimension=1, tiled=True
        ).astype(jnp.float32),
        lax.psum_scatter(
            grad_mod_full.astype(jnp.bfloat16), "tp", scatter_dimension=1, tiled=True
        ).astype(jnp.float32),
    )
    grad_text = jnp.dot(
        caption.T, grad_context.astype(jnp.bfloat16), preferred_element_type=jnp.float32
    )
    grad_bias = jnp.sum(grad_mod, axis=0)
    embed_full = silu_embed.astype(jnp.float32)
    mod_term = jnp.dot(embed_full.T, grad_mod, precision=HIGH)
    summed = (
        lax.psum_scatter(mod_term, "wide", scatter_dimension=1, tiled=True),
        lax.psum_scatter(grad_bias, "wide", scatter_dimension=0, tiled=True),
        lax.psum_scatter(grad_text, "wide", scatter_dimension=0, tiled=True),
        lax.psum_scatter(grad_sqkv, "wide", scatter_dimension=0, tiled=True),
        lax.psum_scatter(grad_so, "wide", scatter_dimension=1, tiled=True),
        lax.psum_scatter(grad_tqkv, "wide", scatter_dimension=0, tiled=True),
        lax.psum_scatter(grad_to, "wide", scatter_dimension=1, tiled=True),
        lax.psum_scatter(grad_cq, "wide", scatter_dimension=0, tiled=True),
        lax.psum_scatter(grad_ckv, "wide", scatter_dimension=0, tiled=True),
        lax.psum_scatter(grad_co, "wide", scatter_dimension=1, tiled=True),
        lax.psum_scatter(grad_fc1, "wide", scatter_dimension=0, tiled=True),
        lax.psum_scatter(grad_fc2, "wide", scatter_dimension=1, tiled=True),
    )
    grad_w_mod = summed[0]
    return (
        block_out,
        grad_tokens,
        grad_w_mod,
        summed[1],
        summed[2],
        summed[3],
        summed[4],
        summed[5],
        summed[6],
        summed[7],
        summed[8],
        summed[9],
        summed[10],
        summed[11],
    )


def solution(mesh):
    placed = (
        P("wide", "tp", None),
        P("wide", "tp", None),
        P("wide", None),
        P(),
        P(),
        P(),
        P(None, "tp"),
        P("tp"),
        P(None, "tp"),
        P(None, None, "tp"),
        P("tp", None),
        P(None, None, "tp"),
        P("tp", None),
        P(None, "tp"),
        P(None, None, "tp"),
        P("tp", None),
        P(None, "tp"),
        P("tp", None),
    )
    return jax.shard_map(
        on_device,
        mesh=mesh,
        in_specs=placed,
        out_specs=(
            P("wide", "tp", None),
            P("wide", "tp", None),
            P(None, ("tp", "wide")),
            P(("tp", "wide")),
            P("wide", "tp"),
            P("wide", None, "tp"),
            P("tp", "wide"),
            P("wide", None, "tp"),
            P("tp", "wide"),
            P("wide", "tp"),
            P("wide", None, "tp"),
            P("tp", "wide"),
            P("wide", "tp"),
            P("tp", "wide"),
        ),
        check_vma=False,
    )
```

profile of v0, /device:TPU:0, one launch (start us, length us, event | category | flops | bytes accessed | tf_op | source)
XLA Modules:
  0.0 2614.6 jit_solution(12079315355009340792)
XLA Ops:
  21.3 11.9 all-gather.11.cloned.1.call-done
  33.2 6.2 convolution_convert_fusion.2
  52.8 9.8 reduce-scatter.37.cloned.1.call-done
  66.5 10.6 all-gather.13.cloned.1.call-done
  77.1 6.2 convolution_convert_fusion.1
  95.6 6.8 all-to-all-start
  102.6 43.1 %all-to-all-done = bf16[2,256,8,216]{3,2,0,1:T(8,128)(2,1)} async-done(((bf16[2,256,8,216]{3,2,0,1:T(8,128)(2,1)}), bf16[2,256,8,216]{3,2,0,1:T(8,128)(2,1)}, u32[]{:S(2)}, u32[]{:S(2)}) %all-to-all-start) | async-done | bytes 1769504 | tf_op jit(solution)/shard_map/all_to_all | solution.py:198
  148.9 8.9 reshape.316
  165.4 36.2 %all_to_all.68 = bf16[32,16,8,72]{3,2,1,0:T(8,128)(2,1)S(1)} all-to-all(bf16[32,16,8,72]{3,2,1,0:T(8,128)(2,1)S(1)} %copy.122), channel_id=1, replica_groups=mesh['wide'=16,'tp'=2] {'wide'}, dimensions={0} | all-to-all | bytes 1179648 | tf_op jit(solution)/shard_map/all_to_all | solution.py:101
  220.8 46.5 %all-gather.1 = bf16[16,15,1152]{2,1,0:T(8,128)(2,1)} all-gather(bf16[1,15,1152]{2,1,0:T(8,128)(2,1)S(1)} %fusion.10), channel_id=1, replica_groups=mesh['wide'=16,'tp'=2] {'wide'}, dimensions={0}, use_global_device_ids=true | all-gather | bytes 587520 | tf_op jit(solution)/shard_map/all_gather | solution.py:169
  301.4 7.7 all-gather.19.cloned.1.call-done
  309.0 8.3 fusion.117
  321.6 11.9 fusion.7
  333.5 7.7 convolution_convert_fusion.6
  341.3 9.0 convolution_convert_fusion.7
  354.5 8.7 reduce-scatter.43.cloned.1.call-done
  367.9 10.5 all-gather.21.cloned.1.call-done
  392.2 9.9 reduce-scatter.47.cloned.1.call-done
  406.8 10.5 all-gather.23.cloned.1.call-done
  426.1 33.8 %all_to_all.69 = bf16[2,256,8,72]{3,2,0,1:T(8,128)(2,1)S(1)} all-to-all(bf16[2,256,8,72]{3,2,0,1:T(8,128)(2,1)} %copy.130), channel_id=1, replica_groups=mesh['wide'=16,'tp'=2] {'wide'}, dimensions={1} | all-to-all | bytes 1179648 | tf_op jit(solution)/shard_map/all_to_all | solution.py:295
  470.7 8.1 reshape.327
  478.8 52.3 %all_to_all.70 = bf16[32,16,8,216]{3,2,1,0:T(8,128)(2,1)S(1)} all-to-all(bf16[32,16,8,216]{3,2,1,0:T(8,128)(2,1)} %reshape.327), channel_id=1, replica_groups=mesh['wide'=16,'tp'=2] {'wide'}, dimensions={0} | all-to-all | bytes 3538944 | tf_op jit(solution)/shard_map/all_to_all | solution.py:105
  532.6 8.9 reshape.328
  541.4 6.8 copy.136
  548.3 6.3 convolution_convert_fusion.4
  555.0 6.6 reduce-scatter.49.cloned.1.call-done
  568.4 10.5 all-gather.25.cloned.1.call-done
  621.2 49.6 %fusion = f32[16,1152]{1,0:T(8,128)S(1)} fusion(f32[240,1152]{1,0:T(8,128)} %reshape.332), kind=kCustom, calls=%all-reduce-scatter | all-reduce-scatter fusion | flops 294913 | bytes 1180160
  687.2 11.5 copy.149
  720.2 9.8 fusion.108
  730.0 9.1 fusion.124
  739.6 5.8 convolution_bitcast_fusion
  745.5 11.2 copy.146
  758.7 6.1 fusion.120
  769.8 6.1 fusion.118
  776.6 9.0 fusion.102
  786.9 122.5 %all-reduce.11.cloned.1.call-done = f32[1152,2,576]{2,1,0:T(2,128)} async-done(((f32[1152,2,576]{2,1,0:T(2,128)}), f32[1152,2,576]{2,1,0:T(2,128)}) %all-reduce.11.cloned.1.call-update) | async-done | bytes 5308432
  915.4 75.2 %all-reduce.1 = f32[3456]{0:T(1024)S(1)} all-reduce(f32[3456]{0:T(1024)S(1)} %convert_reduce_fusion.5), channel_id=12, replica_groups=mesh['wide'=16,'tp'=2] {'wide'}, use_global_device_ids=true, to_apply=%region_42.43.clone | all-reduce | flops 3456 | bytes 27648
  991.3 53.7 %reduce-scatter.75.cloned.1.call-done = f32[576,72]{0,1:T(8,128)} async-done(((f32[576,1152]{0,1:T(8,128)}), f32[576,72]{0,1:T(8,128)}) %reduce-scatter.75.cloned.1.call-update) | async-done | bytes 165904
  1044.9 135.4 %reduce-scatter.73.cloned.1.call-done = f32[72,576]{1,0:T(8,128)} async-done(((f32[1152,576]{1,0:T(8,128)}), f32[72,576]{1,0:T(8,128)}) %reduce-scatter.73.cloned.1.call-update) | async-done | bytes 165904
  1180.4 135.3 %reduce-scatter.71.cloned.1.call-done = f32[576,72]{0,1:T(8,128)} async-done(((f32[576,1152]{0,1:T(8,128)}), f32[576,72]{0,1:T(8,128)}) %reduce-scatter.71.cloned.1.call-update) | async-done | bytes 165904
  1315.7 135.3 %reduce-scatter.69.cloned.1.call-done = f32[576,72]{0,1:T(8,128)} async-done(((f32[576,1152]{0,1:T(8,128)}), f32[576,72]{0,1:T(8,128)}) %reduce-scatter.69.cloned.1.call-update) | async-done | bytes 165904
  1451.0 188.5 %reduce-scatter.61.cloned.1.call-done = f32[2304,72]{0,1:T(8,128)} async-done(((f32[2304,1152]{0,1:T(8,128)}), f32[2304,72]{0,1:T(8,128)}) %reduce-scatter.61.cloned.1.call-update) | async-done | bytes 663568 | tf_op jit(solution)/shard_map/reduce_scatter | solution.py:388
  1639.6 187.8 %reduce-scatter.59.cloned.1.call-done = f32[72,2304]{1,0:T(8,128)} async-done(((f32[1152,2304]{1,0:T(8,128)}), f32[72,2304]{1,0:T(8,128)}) %reduce-scatter.59.cloned.1.call-update) | async-done | bytes 663568 | tf_op jit(solution)/shard_map/reduce_scatter | solution.py:387
  1827.3 178.2 %reduce-scatter.53.cloned.1.call-done = f32[256,576]{0,1:T(8,128)} async-done(((f32[4096,576]{0,1:T(8,128)}), f32[256,576]{0,1:T(8,128)}) %reduce-scatter.53.cloned.1.call-update) | async-done | bytes 589840 | tf_op jit(solution)/shard_map/reduce_scatter | solution.py:379
  2005.5 172.4 %reduce-scatter.57.cloned.1.call-done = f32[72,3,576]{2,0,1:T(8,128)} async-done(((f32[1152,3,576]{2,0,1:T(8,128)}), f32[72,3,576]{2,0,1:T(8,128)}) %reduce-scatter.57.cloned.1.call-update) | async-done | bytes 497680 | tf_op jit(solution)/shard_map/reduce_scatter | solution.py:382
  2177.9 172.4 %reduce-scatter.55.cloned.1.call-done = f32[72,3,576]{2,0,1:T(8,128)} async-done(((f32[1152,3,576]{2,0,1:T(8,128)}), f32[72,3,576]{2,0,1:T(8,128)}) %reduce-scatter.55.cloned.1.call-update) | async-done | bytes 497680 | tf_op jit(solution)/shard_map/reduce_scatter | solution.py:380
  2350.3 257.6 %reduce-scatter.67.cloned.1.call-done = f32[1152,216]{0,1:T(8,128)} async-done(((f32[1152,3456]{0,1:T(8,128)}), f32[1152,216]{0,1:T(8,128)}) %reduce-scatter.67.cloned.1.call-update) | async-done | bytes 995344
  (374 shorter events, 261.0 us)
Async XLA Ops:
  7.2 212.7 %copy-start = (bf16[1152,2,576]{0,2,1:T(8,128)(2,1)S(1)}, bf16[1152,2,576]{0,2,1:T(8,128)(2,1)}, u32[]{:S(2)}) copy-start(bf16[1152,2,576]{0,2,1:T(8,128)(2,1)} %param.32) | copy-start | bytes 7962628
  7.2 26.0 all-gather.11.cloned.1.call-start
  9.3 10.2 copy-start.48
  10.7 8.8 copy-start.55
  11.6 8.5 copy-start.4
  21.2 41.3 %reduce-scatter.37.cloned.1.call-start = ((), (), s32[]{:S(2)}) async-start(), calls=%async_computation.25 | async-start | bytes 1769472 | tf_op jit(solution)/shard_map/reduce_scatter | solution.py:85
  52.5 24.6 all-gather.13.cloned.1.call-start
  65.4 17.9 copy-start.57
  95.6 50.1 %all-to-all-start = ((bf16[2,256,8,216]{3,2,0,1:T(8,128)(2,1)}), bf16[2,256,8,216]{3,2,0,1:T(8,128)(2,1)}, u32[]{:S(2)}, u32[]{:S(2)}) async-start(bf16[2,256,8,216]{3,2,0,1:T(8,128)(2,1)} %copy.117), calls=%async_computation.1 | async-start | bytes 4194304 | tf_op jit(solution)/shard_map/all_to_all | solution.py:198
  102.4 113.8 %reduce-scatter.39.cloned.1.call-start = ((), (), s32[]{:S(2)}) async-start(), calls=%async_computation.27 | async-start | bytes 1769472 | tf_op jit(solution)/shard_map/reduce_scatter | solution.py:85
  209.1 69.8 %all-gather.15.cloned.1.call-start = ((), (), s32[]{:S(2)}) async-start(), calls=%async_computation.28 | async-start | bytes 1769472 | tf_op jit(solution)/shard_map/all_gather | solution.py:81
  217.8 186.3 %copy-start.46 = (f32[2,128]{1,0:T(2,128)}, f32[2,128]{1,0:T(2,128)S(1)}, u32[]{:S(2)}) copy-start(f32[2,128]{1,0:T(2,128)S(1)} %broadcast_multiply_fusion.9) | copy-start | bytes 3076
  219.9 76.5 %reduce-scatter.41.cloned.1.call-start = ((), (), s32[]{:S(2)}) async-start(), calls=%async_computation.29 | async-start | bytes 1769472 | tf_op jit(solution)/shard_map/reduce_scatter | solution.py:85
  220.8 52.9 %copy-start.67 = (s32[2]{0:T(128)S(1)}, s32[2]{0:T(128)}, u32[]{:S(2)}) copy-start(s32[2]{0:T(128)} %get-tuple-element.36) | copy-start | bytes 28
  220.8 52.9 %copy-start.1 = (s32[2]{0:T(128)S(1)}, s32[2]{0:T(128)}, u32[]{:S(2)}) copy-start(s32[2]{0:T(128)} %param.21) | copy-start | bytes 28
  291.7 17.3 all-gather.19.cloned.1.call-start
  293.8 27.9 %all-gather.17.cloned.1.call-start = ((), (), s32[]{:S(2)}) async-start(), calls=%async_computation.30 | async-start | bytes 1769472 | tf_op jit(solution)/shard_map/all_gather | solution.py:81
  300.9 50.3 %reduce-scatter.45.cloned.1.call-start = ((), (), s32[]{:S(2)}) async-start(), calls=%async_computation.33 | async-start | bytes 1769472 | tf_op jit(solution)/shard_map/reduce_scatter | solution.py:95
  333.5 7.7 copy-start.75
  341.2 22.0 reduce-scatter.43.cloned.1.call-start
  350.3 28.1 %all-gather.21.cloned.1.call-start = ((), (), s32[]{:S(2)}) async-start(), calls=%async_computation.34 | async-start | bytes 1769472 | tf_op jit(solution)/shard_map/all_gather | solution.py:91
  367.8 34.3 %reduce-scatter.47.cloned.1.call-start = ((), (), s32[]{:S(2)}) async-start(), calls=%async_computation.35 | async-start | bytes 1769472 | tf_op jit(solution)/shard_map/reduce_scatter | solution.py:95
  389.9 12.2 copy-start.53
  392.2 25.1 all-gather.23.cloned.1.call-start
  406.7 155.0 %reduce-scatter.49.cloned.1.call-start = ((), (), s32[]{:S(2)}) async-start(), calls=%async_computation.37 | async-start | bytes 1769472 | tf_op jit(solution)/shard_map/reduce_scatter | solution.py:95
  426.1 34.9 %copy-start.9 = (f32[16,8,32,32]{2,3,1,0:T(8,128)S(1)}, f32[16,8,32,32]{2,3,1,0:T(8,128)}, u32[]{:S(2)}) copy-start(f32[16,8,32,32]{2,3,1,0:T(8,128)} %copy-done.8) | copy-start | bytes 1572868
  548.3 13.4 copy-start.51
  548.3 13.4 copy-start.58
  554.6 9.1 copy-start.47
  554.6 9.1 copy-start.60
  554.6 24.3 all-gather.25.cloned.1.call-start
  568.3 111.0 %reduce-scatter.51.cloned.1.call-start = ((), (), s32[]{:S(2)}) async-start(), calls=%async_computation.39 | async-start | bytes 1769472 | tf_op jit(solution)/shard_map/reduce_scatter | solution.py:95
  600.1 139.5 %reduce-scatter.65.cloned.1.call-start = ((), (), s32[]{:S(2)}) async-start(), calls=%async_computation.46 | async-start | bytes 442368
  618.0 54.8 %copy-start.68 = (u32[32]{0:T(128)S(1)}, u32[32]{0:T(128)}, u32[]{:S(2)}) copy-start(u32[32]{0:T(128)} %constant.97) | copy-start | bytes 388
  670.8 3.4 collective-permute-start
  679.2 97.0 %reduce-scatter.63.cloned.1.call-start = ((), (), s32[]{:S(2)}) async-start(), calls=%async_computation.45 | async-start | bytes 2654208
  683.8 225.5 %all-reduce.11.cloned.1.call-start = ((), (), s32[]{:S(2)}) async-start(), calls=%async_computation.47 | async-start | bytes 11796480
  698.7 346.3 %reduce-scatter.75.cloned.1.call-start = ((), (), s32[]{:S(2)}) async-start(), calls=%async_computation.52 | async-start | bytes 3133440
  703.4 477.0 %reduce-scatter.73.cloned.1.call-start = ((), (), s32[]{:S(2)}) async-start(), calls=%async_computation.51 | async-start | bytes 3133440
  708.4 607.3 %reduce-scatter.71.cloned.1.call-start = ((), (), s32[]{:S(2)}) async-start(), calls=%async_computation.50 | async-start | bytes 3133440
  715.4 735.6 %reduce-scatter.69.cloned.1.call-start = ((), (), s32[]{:S(2)}) async-start(), calls=%async_computation.49 | async-start | bytes 3133440
  720.1 919.4 %reduce-scatter.61.cloned.1.call-start = ((), (), s32[]{:S(2)}) async-start(), calls=%async_computation.44 | async-start | bytes 11280384 | tf_op jit(solution)/shard_map/reduce_scatter | solution.py:388
  730.0 1097.4 %reduce-scatter.59.cloned.1.call-start = ((), (), s32[]{:S(2)}) async-start(), calls=%async_computation.43 | async-start | bytes 11280384 | tf_op jit(solution)/shard_map/reduce_scatter | solution.py:387
  739.1 1266.4 %reduce-scatter.53.cloned.1.call-start = ((), (), s32[]{:S(2)}) async-start(), calls=%async_computation.40 | async-start | bytes 10027008 | tf_op jit(solution)/shard_map/reduce_scatter | solution.py:379
  745.5 1432.5 %reduce-scatter.57.cloned.1.call-start = ((), (), s32[]{:S(2)}) async-start(), calls=%async_computation.42 | async-start | bytes 9400320 | tf_op jit(solution)/shard_map/reduce_scatter | solution.py:382
  764.8 1585.5 %reduce-scatter.55.cloned.1.call-start = ((), (), s32[]{:S(2)}) async-start(), calls=%async_computation.41 | async-start | bytes 9400320 | tf_op jit(solution)/shard_map/reduce_scatter | solution.py:380
  776.0 1831.9 %reduce-scatter.67.cloned.1.call-start = ((), (), s32[]{:S(2)}) async-start(), calls=%async_computation.48 | async-start | bytes 16920576
  785.6 125.6 %copy-start.66 = (f32[2,128]{1,0:T(2,128)S(1)}, f32[2,128]{1,0:T(2,128)}, u32[]{:S(2)}) copy-start(f32[2,128]{1,0:T(2,128)} %get-tuple-element.17) | copy-start | bytes 3076
  (59 other events, 148.4 us)
Sparse Core Ops, SparseCore 0:
  21.3 11.7 all-gather.10
  52.7 9.8 reduce-scatter.36
  66.7 10.4 all-gather.12
  209.2 6.9 reduce-scatter.38
  220.0 10.4 all-gather.14
  291.8 4.5 reduce-scatter.40
  298.6 10.3 all-gather.18
  311.2 10.3 all-gather.16
  341.3 9.8 reduce-scatter.44
  353.3 9.8 reduce-scatter.42
  367.9 10.4 all-gather.20
  392.3 9.8 reduce-scatter.46
  406.9 10.4 all-gather.22
  554.7 6.9 reduce-scatter.48
  568.4 10.3 all-gather.24
  600.2 9.8 reduce-scatter.50
  679.3 6.7 reduce-scatter.64
  688.2 10.4 reduce-scatter.62
  706.1 203.2 all-reduce.10
  915.6 129.2 reduce-scatter.74
  1051.3 129.0 reduce-scatter.72
  1186.8 128.8 reduce-scatter.70
  1322.1 128.8 reduce-scatter.68
  1458.3 181.2 reduce-scatter.60
  1646.0 181.3 reduce-scatter.58
  1834.4 171.0 reduce-scatter.52
  2011.6 166.2 reduce-scatter.56
  2184.2 166.0 reduce-scatter.54
  2356.7 251.1 reduce-scatter.66
where the time goes:
time: 2630 us; the launch traced here: 2610 us
  waiting for transfers between devices  1890 us (72%)
  blocking collectives  297 us (11%)
  matrix products  181 us (7%)
  local copies, waits for them, and re-layouts  168 us (6%)
  other arithmetic  50.1 us (2%)
    unnamed x38, waiting for transfers between devices  840 us
    reduce_scatter x1, waiting for transfers between devices, on_device(): lax.psum_scatter(grad_fc2, 'wide', scatter_dimension=1, tiled=True)  189 us
    reduce_scatter x1, waiting for transfers between devices, on_device(): lax.psum_scatter(grad_fc1, 'wide', scatter_dimension=0, tiled=True)  188 us
    reduce_scatter x1, waiting for transfers between devices, on_device(): lax.psum_scatter(grad_text, 'wide', scatter_dimension=0, tiled=True)  178 us
    reduce_scatter x1, waiting for transfers between devices, on_device(): lax.psum_scatter(grad_tqkv, 'wide', scatter_dimension=0, tiled=True)  172 us
    reduce_scatter x1, waiting for transfers between devices, on_device(): lax.psum_scatter(grad_sqkv, 'wide', scatter_dimension=0, tiled=True)  172 us
    unnamed x2, blocking collectives  125 us
  transfers between devices with their start and end apart: 31, of which 26 were waited for; matrix products, arithmetic and copies ran while one was open for 9% of the time, Pallas kernels for 0%

commit v1 on v0

v1 whole, which is shorter than its diff:
```python
import math

import jax
import jax.numpy as jnp
from jax import lax
from jax.sharding import PartitionSpec as P

HD = 72
LTXT = 120
EPS = 1e-06
NEGATIVE = -1e30
HIGH = lax.Precision.HIGHEST
BF = jnp.bfloat16
F32 = jnp.float32


def dot32(left, right):
    return jnp.dot(left, right, preferred_element_type=F32)


def dot_nt(left, right):
    return lax.dot_general(left, right, (((1,), (1,)), ((), ())), preferred_element_type=F32)


def dot_tn(left, right):
    return lax.dot_general(left, right, (((0,), (0,)), ((), ())), preferred_element_type=F32)


def layer_norm(operand):
    average = jnp.mean(operand, axis=-1, keepdims=True)
    centred = operand - average
    spread = jnp.mean(centred * centred, axis=-1, keepdims=True)
    inverse = lax.rsqrt(spread + EPS)
    return (centred * inverse, inverse)


def norm_back(grad_normed, normed, inverse):
    grad_mean = jnp.mean(grad_normed, axis=-1, keepdims=True)
    grad_cross = jnp.mean(grad_normed * normed, axis=-1, keepdims=True)
    return inverse * (grad_normed - grad_mean - normed * grad_cross)


def gelu_tanh(operand):
    return jax.nn.gelu(operand, approximate=True)


def attend_forward(queries, key_rows, value_rows, allowed):
    scores = jnp.einsum("...qd,...kd->...qk", queries, key_rows, preferred_element_type=F32)
    scores = scores * HD ** (-0.5)
    if allowed is not None:
        scores = jnp.where(allowed, scores, NEGATIVE)
    largest = jnp.max(scores, axis=-1, keepdims=True)
    log_total = largest + jnp.log(jnp.sum(jnp.exp(scores - largest), axis=-1, keepdims=True))
    attn_probs = jnp.exp(scores - log_total).astype(BF)
    output = jnp.einsum("...qk,...kd->...qd", attn_probs, value_rows, preferred_element_type=F32)
    return (output.astype(BF), log_total)


def attend_backward(queries, key_rows, value_rows, log_total, grad_out, allowed):
    factor = HD ** (-0.5)
    scores = jnp.einsum("...qd,...kd->...qk", queries, key_rows, preferred_element_type=F32)
    scores = scores * factor
    if allowed is not None:
        scores = jnp.where(allowed, scores, NEGATIVE)
    attn_probs = jnp.exp(scores - log_total)
    grad_probs = jnp.einsum("...qd,...kd->...qk", grad_out, value_rows, preferred_element_type=F32)
    row_dot = jnp.sum(attn_probs * grad_probs, axis=-1, keepdims=True)
    grad_scores = (attn_probs * (grad_probs - row_dot)).astype(BF)
    grad_queries = (
        jnp.einsum("...qk,...kd->...qd", grad_scores, key_rows, preferred_element_type=F32) * factor
    )
    grad_keys = (
        jnp.einsum("...qk,...qd->...kd", grad_scores, queries, preferred_element_type=F32) * factor
    )
    grad_values = jnp.einsum(
        "...qk,...qd->...kd", attn_probs.astype(BF), grad_out, preferred_element_type=F32
    )
    return (grad_queries, grad_keys, grad_values)


def tp_from(operand, shift):
    size = lax.axis_size("tp")
    return lax.ppermute(operand, "tp", [(s, (s - shift) % size) for s in range(size)])


def tp_to(operand, shift):
    size = lax.axis_size("tp")
    return lax.ppermute(operand, "tp", [(s, (s + shift) % size) for s in range(size)])


def tp_gather(operand):
    return [operand] + [tp_from(operand, k) for k in range(1, lax.axis_size("tp"))]


def tp_sum(parts):
    total = parts[0].astype(F32)
    for k in range(1, lax.axis_size("tp")):
        total = total + tp_to(parts[k].astype(BF), k).astype(F32)
    return total


def tp_ordered(relative):
    size = lax.axis_size("tp")
    start = (size - lax.axis_index("tp")) % size
    return lax.dynamic_slice_in_dim(jnp.stack(relative + relative), start, size, axis=0)


def flip(operand, mask):
    size = lax.axis_size("wide")
    return lax.ppermute(operand, "wide", [(s, s ^ mask) for s in range(size)])


def pick(operand, index, axis):
    return lax.dynamic_index_in_dim(operand, index, axis, keepdims=False)


def exchange_halves(sides, bit):
    mine = (lax.axis_index("wide") >> bit) & 1
    keep = [pick(side, mine, -2) for side in sides]
    give = [pick(side, 1 - mine, -2) for side in sides]
    return keep, [flip(side, 1 << bit) for side in give]


def weight_grad(pairs, first):
    wide = lax.axis_index("wide")
    second = 1 - first
    depth = lax.axis_size("wide") // 4
    total = None
    for model_side, head_side in pairs:
        term = dot_tn(model_side, head_side)
        total = term if total is None else total + term
    columns = total.shape[1]
    total = total.astype(BF).reshape(depth, 2, 2, total.shape[0] // (4 * depth), columns)
    axis = 1 if second == 1 else 2
    mine = (wide >> second) & 1
    half = pick(total, mine, axis).astype(F32) + flip(
        pick(total, 1 - mine, axis), 1 << second
    ).astype(F32)
    at = wide >> 2
    block = pick(half, at, 0)
    narrow = half.astype(BF)
    for k in range(1, depth):
        block = block + flip(pick(narrow, at ^ k, 0), 4 * k).astype(F32)
    mine = (wide >> first) & 1
    keep = pick(block, mine, 0)
    got = flip(pick(block, 1 - mine, 0).astype(BF), 1 << first).astype(F32)
    return jnp.where(mine == 0, jnp.stack([keep, got], axis=1), jnp.stack([got, keep], axis=1))


def paired_tokens(model_side, head_sides, first):
    stack = jnp.stack(head_sides)
    (keep,), (got,) = exchange_halves([stack], first)
    keep = keep.reshape(keep.shape[0], keep.shape[1], -1)
    got = got.reshape(keep.shape)
    model_got = flip(model_side, 1 << first)
    pairs = [(model_side, keep[0]), (model_got, got[0])]
    for k in range(1, lax.axis_size("tp")):
        pairs.append((tp_to(model_side, k), tp_to(keep[k], k)))
        pairs.append((tp_to(model_got, k), tp_to(got[k], k)))
    return pairs


def on_device(
    tokens,
    cotangent,
    caption,
    caption_len,
    clip_id,
    timestep,
    w_mod,
    b_mod,
    w_text,
    w_sqkv,
    w_so,
    w_tqkv,
    w_to,
    w_cq,
    w_ckv,
    w_co,
    w_fc1,
    w_fc2,
):
    n_tp = lax.axis_size("tp")
    n_wide = lax.axis_size("wide")
    frames_here, patch_part, width = tokens.shape
    local_cols = w_so.shape[0]
    heads_here = local_cols // HD
    hidden = w_fc1.shape[1]
    clip_count = timestep.shape[0]
    frames = clip_id.shape[0]
    patch_here = patch_part // n_wide
    rows = frames_here * patch_part
    wide_at = lax.axis_index("wide")

    def qkv_rows(weight):
        return weight.transpose(1, 2, 0)

    tqkv_all = tp_gather(qkv_rows(w_tqkv))
    to_all = tp_gather(w_to)
    cq_all = tp_gather(w_cq.T)
    co_all = tp_gather(w_co)
    fc1_all = tp_gather(w_fc1)
    fc2_all = tp_gather(w_fc2)

    half_width = width // 2
    frequencies = jnp.exp(-math.log(10000.0) * jnp.arange(half_width).astype(F32) / half_width)
    angles = timestep.astype(F32)[:, None] * frequencies[None, :]
    embedding = jnp.concatenate([jnp.cos(angles), jnp.sin(angles)], axis=1)
    silu_embed = jax.nn.silu(embedding).astype(BF)
    mod_part = (dot32(silu_embed, w_mod) + b_mod.astype(F32)).astype(BF)
    modulation = tp_ordered(tp_gather(mod_part)).transpose(1, 0, 2).reshape(clip_count, -1)
    my_clips = lax.dynamic_slice_in_dim(clip_id, wide_at * frames_here, frames_here)
    clip_hot = (clip_id[:, None] == jnp.arange(clip_count)[None, :]).astype(BF)
    mod_frames = dot32(clip_hot, modulation)
    mod_here = lax.dynamic_slice_in_dim(mod_frames, wide_at * frames_here, frames_here)
    here = [mod_here[:, None, i * width : (i + 1) * width] for i in range(3)]
    every = [mod_frames[:, None, i * width : (i + 1) * width] for i in range(3, 6)]
    shift_one, scale_one, gate_one = here
    shift_two, scale_two, gate_two = every

    context_part = dot32(caption, w_text).astype(BF)
    context = tp_ordered(tp_gather(context_part)).transpose(1, 0, 2).reshape(caption.shape[0], -1)
    ckv_rows = w_ckv.transpose(1, 2, 0).reshape(2 * local_cols, width)
    keyval_part = dot_nt(context, ckv_rows).astype(BF)
    keyval = lax.all_gather(keyval_part, "wide", axis=0, tiled=True)
    keyval_all = tp_gather(keyval)
    text_cols = caption.shape[1] // n_wide
    context_cols = width // n_wide
    for_owner = jnp.concatenate(
        [
            caption.reshape(-1, n_wide, text_cols),
            context.reshape(-1, n_wide, context_cols),
        ],
        axis=2,
    ).transpose(1, 0, 2)
    for_owner = lax.all_to_all(for_owner, "wide", split_axis=0, concat_axis=0, tiled=True)
    for_owner = for_owner.reshape(-1, text_cols + context_cols)
    caption_cols, context_cols = for_owner[:, :text_cols], for_owner[:, text_cols:]

    def to_patches(operand):
        operand = operand.reshape(frames_here, n_wide, patch_here, width).transpose(1, 0, 2, 3)
        operand = lax.all_to_all(operand, "wide", split_axis=0, concat_axis=0, tiled=True)
        return operand.reshape(frames, patch_here, width)

    def to_frames(operand):
        operand = operand.reshape(n_wide, frames_here, patch_here, width)
        operand = lax.all_to_all(operand, "wide", split_axis=0, concat_axis=0, tiled=True)
        return operand.transpose(1, 0, 2, 3).reshape(frames_here, patch_part, width)

    grad_out = to_patches(cotangent).astype(F32)

    tokens_all = jnp.stack(tp_gather(tokens)).astype(F32)
    normed_one, inverse_one = layer_norm(tokens_all)
    h_one = (normed_one * (1.0 + scale_one) + shift_one).astype(BF)
    normed_one, inverse_one = normed_one[0], inverse_one[0]
    h_one_rows = h_one.reshape(n_tp * rows, width)
    sqkv_rows = qkv_rows(w_sqkv)

    def spatial_heads(operand):
        return (
            operand.reshape(n_tp, frames_here, patch_part, heads_here, HD)
            .transpose(1, 3, 0, 2, 4)
            .reshape(frames_here, heads_here, n_tp * patch_part, HD)
        )

    def spatial_rows(operand):
        return (
            operand.reshape(frames_here, heads_here, n_tp, patch_part, HD)
            .transpose(2, 0, 3, 1, 4)
            .reshape(n_tp * rows, local_cols)
        )

    heads_one = [spatial_heads(dot_nt(h_one_rows, sqkv_rows[i]).astype(BF)) for i in range(3)]
    out_one, total_one = attend_forward(*heads_one, None)
    attn_one = spatial_rows(out_one)
    y_one = tp_sum(dot32(attn_one, w_so).reshape(n_tp, frames_here, patch_part, width))
    stream_one = (tokens.astype(F32) + gate_one * y_one).astype(BF)

    count = frames * patch_here
    stream = to_patches(stream_one).astype(F32)
    clip_rows = jnp.repeat(clip_id, patch_here)
    patch_rows = jnp.tile(jnp.arange(patch_here), frames)
    allowed_two = (clip_rows[:, None] == clip_rows[None, :]) & (
        patch_rows[:, None] == patch_rows[None, :]
    )
    key_clip = jnp.repeat(jnp.arange(clip_count), LTXT)
    key_at = jnp.tile(jnp.arange(LTXT), clip_count)
    allowed_three = (clip_rows[:, None] == key_clip[None, :]) & (
        key_at < jnp.repeat(caption_len, LTXT)
    )[None, :]

    def heads(operand):
        return operand.reshape(-1, heads_here, HD).transpose(1, 0, 2)

    def unheads(operand):
        return operand.transpose(1, 0, 2).reshape(-1, local_cols)

    stream = stream.reshape(count, width)
    normed_two, inverse_two = layer_norm(stream)
    h_two = normed_two.astype(BF)
    heads_two = [
        [heads(dot_nt(h_two, weight[i]).astype(BF)) for i in range(3)] for weight in tqkv_all
    ]
    kept_two = [attend_forward(*part, allowed_two) for part in heads_two]
    attn_two = [unheads(part[0]) for part in kept_two]
    stream = stream + sum(dot32(part, weight) for part, weight in zip(attn_two, to_all))

    normed_three, inverse_three = layer_norm(stream)
    h_three = normed_three.astype(BF)
    heads_three = []
    for r in range(n_tp):
        query = heads(dot_nt(h_three, cq_all[r]).astype(BF))
        key_rows = heads(keyval_all[r][:, :local_cols])
        value_rows = heads(keyval_all[r][:, local_cols:])
        heads_three.append((query, key_rows, value_rows))
    kept_three = [attend_forward(*part, allowed_three) for part in heads_three]
    attn_three = [unheads(part[0]) for part in kept_three]
    stream = stream + sum(dot32(part, weight) for part, weight in zip(attn_three, co_all))

    def by_frame(operand):
        return operand.reshape(frames, patch_here, -1)

    def by_row(operand):
        return operand.reshape(count, -1)

    normed_four, inverse_four = layer_norm(stream)
    h_four = by_row((by_frame(normed_four) * (1.0 + scale_two) + shift_two)).astype(BF)
    upper = [dot32(h_four, weight) for weight in fc1_all]
    active = [gelu_tanh(part).astype(BF) for part in upper]
    y_four = sum(dot32(part, weight) for part, weight in zip(active, fc2_all))
    block_out = (by_frame(stream) + gate_two * by_frame(y_four)).astype(BF)
    block_out = to_frames(block_out)

    def clip_sums(operand, hot):
        return lax.dot_general(
            hot, jnp.sum(operand, axis=1), (((0,), (0,)), ((), ())), precision=HIGH
        )

    hot_all = clip_hot.astype(F32)
    hot_here = lax.dynamic_slice_in_dim(hot_all, wide_at * frames_here, frames_here)

    grad_gate_two = clip_sums(grad_out * by_frame(y_four), hot_all)
    grad_y4 = by_row(gate_two * grad_out).astype(BF)
    grad_upper = []
    for r in range(n_tp):
        unused, gelu_back = jax.vjp(gelu_tanh, upper[r])
        grad_upper.append(gelu_back(dot_nt(grad_y4, fc2_all[r]))[0].astype(BF))
    grad_h4 = sum(dot_nt(part, weight) for part, weight in zip(grad_upper, fc1_all))
    grad_shift_two = clip_sums(by_frame(grad_h4), hot_all)
    grad_scale_two = clip_sums(by_frame(grad_h4 * normed_four), hot_all)
    grad_normed = by_row(by_frame(grad_h4) * (1.0 + scale_two))
    grad = by_row(grad_out) + norm_back(grad_normed, normed_four, inverse_four)

    def halves(parts, groups):
        return [part.reshape(part.shape[0], groups, 2, -1) for part in parts]

    grad_fc2 = weight_grad(paired_tokens(grad_y4, halves(active, 1), 1), 1)
    grad_fc1 = weight_grad(paired_tokens(h_four, halves(grad_upper, 1), 0), 0)

    grad_y3 = grad.astype(BF)
    grad_co = weight_grad(paired_tokens(grad_y3, halves(attn_three, 1), 1), 1)
    grad_q3, grad_kv = [], []
    for r in range(n_tp):
        grad_attn = heads(dot_nt(grad_y3, co_all[r]).astype(BF))
        grads = attend_backward(*heads_three[r], kept_three[r][1], grad_attn, allowed_three)
        grad_q3.append(unheads(grads[0]).astype(BF))
        grad_kv.append(jnp.concatenate([unheads(grads[1]), unheads(grads[2])], axis=1))
    grad_cq = weight_grad(paired_tokens(h_three, halves(grad_q3, 1), 0), 0)
    grad_h3 = sum(dot32(part, weight) for part, weight in zip(grad_q3, cq_all))
    grad = grad + norm_back(grad_h3, normed_three, inverse_three)
    grad_kv = lax.psum(tp_sum(grad_kv), "wide").astype(BF)
    grad_ckv = dot_tn(context_cols, grad_kv).reshape(-1, 2, local_cols)
    grad_context = dot32(grad_kv, ckv_rows)
    relative = [
        pick(
            grad_context.reshape(-1, n_tp, width // n_tp),
            (lax.axis_index("tp") + k) % n_tp,
            1,
        )
        for k in range(n_tp)
    ]
    grad_context = tp_sum(relative).astype(BF)
    grad_text = dot_tn(caption_cols, grad_context)

    grad_y2 = grad.astype(BF)
    grad_to = weight_grad(paired_tokens(grad_y2, halves(attn_two, 1), 1), 1)
    grad_qkv2 = []
    for r in range(n_tp):
        grad_attn = heads(dot_nt(grad_y2, to_all[r]).astype(BF))
        grads = attend_backward(*heads_two[r], kept_two[r][1], grad_attn, allowed_two)
        grad_qkv2.append(jnp.stack([unheads(part).astype(BF) for part in grads], axis=1))
    grad_tqkv = weight_grad(
        paired_tokens(h_two, [part.reshape(count, 3, 2, -1) for part in grad_qkv2], 0), 0
    )
    grad_h2 = sum(
        dot32(part[:, i], weight[i])
        for part, weight in zip(grad_qkv2, tqkv_all)
        for i in range(3)
    )
    grad = grad + norm_back(grad_h2, normed_two, inverse_two)
    grad = to_frames(by_frame(grad.astype(BF))).astype(F32)

    grad_gate_one = clip_sums(grad * y_one, hot_here)
    grad_y1 = (gate_one * grad).astype(BF)
    grad_y1_rows = jnp.stack(tp_gather(grad_y1)).reshape(n_tp * rows, width)
    grad_attn1 = spatial_heads(dot_nt(grad_y1_rows, w_so).astype(BF))
    grads_one = attend_backward(*heads_one, total_one, grad_attn1, None)
    grad_qkv1 = jnp.stack([spatial_rows(part).astype(BF) for part in grads_one], axis=1)
    grad_h1 = sum(dot32(grad_qkv1[:, i], sqkv_rows[i]) for i in range(3))
    grad_h1 = tp_sum(grad_h1.reshape(n_tp, frames_here, patch_part, width))
    grad_shift_one = clip_sums(grad_h1, hot_here)
    grad_scale_one = clip_sums(grad_h1 * normed_one, hot_here)
    grad = grad + norm_back(grad_h1 * (1.0 + scale_one), normed_one, inverse_one)
    grad_tokens = grad.astype(BF)

    def spatial_pairs(model_rows, own_rows, head_side, first):
        (keep,), (got,) = exchange_halves([head_side], first)
        keep, got = (side.reshape(side.shape[0], -1) for side in (keep, got))
        model_got = jnp.concatenate(tp_gather(flip(own_rows, 1 << first)))
        return [(model_rows, keep), (model_got, got)]

    grad_so = weight_grad(
        spatial_pairs(
            grad_y1_rows, grad_y1.reshape(rows, width), halves([attn_one], 1)[0], 1
        ),
        1,
    )
    grad_sqkv = weight_grad(
        spatial_pairs(
            h_one_rows,
            h_one[0].reshape(rows, width),
            grad_qkv1.reshape(n_tp * rows, 3, 2, -1),
            0,
        ),
        0,
    )

    grad_mod = jnp.concatenate(
        [
            grad_shift_one,
            grad_scale_one,
            grad_gate_one,
            grad_shift_two,
            grad_scale_two,
            grad_gate_two,
        ],
        axis=1,
    )
    grad_mod = lax.psum_scatter(grad_mod, ("tp", "wide"), scatter_dimension=1, tiled=True)
    grad_w_mod = lax.dot_general(
        silu_embed.astype(F32), grad_mod, (((0,), (0,)), ((), ())), precision=HIGH
    )

    def plain(block):
        return block.reshape(block.shape[0], -1)

    def triple(block):
        return block.reshape(block.shape[0], 2, 3, -1).transpose(0, 2, 1, 3).reshape(
            block.shape[0], 3, local_cols
        )

    return (
        block_out,
        grad_tokens,
        grad_w_mod,
        jnp.sum(grad_mod, axis=0),
        grad_text,
        triple(grad_sqkv),
        plain(grad_so).T,
        triple(grad_tqkv),
        plain(grad_to).T,
        plain(grad_cq),
        grad_ckv,
        plain(grad_co).T,
        plain(grad_fc1),
        plain(grad_fc2).T,
    )


def solution(mesh):
    placed = (
        P("wide", "tp", None),
        P("wide", "tp", None),
        P("wide", None),
        P(),
        P(),
        P(),
        P(None, "tp"),
        P("tp"),
        P(None, "tp"),
        P(None, None, "tp"),
        P("tp", None),
        P(None, None, "tp"),
        P("tp", None),
        P(None, "tp"),
        P(None, None, "tp"),
        P("tp", None),
        P(None, "tp"),
        P("tp", None),
    )
    return jax.shard_map(
        on_device,
        mesh=mesh,
        in_specs=placed,
        out_specs=(
            P("wide", "tp", None),
            P("wide", "tp", None),
            P(None, ("tp", "wide")),
            P(("tp", "wide")),
            P("wide", "tp"),
            P("wide", None, "tp"),
            P("tp", "wide"),
            P("wide", None, "tp"),
            P("tp", "wide"),
            P("wide", "tp"),
            P("wide", None, "tp"),
            P("tp", "wide"),
            P("wide", "tp"),
            P("tp", "wide"),
        ),
        check_vma=False,
    )
```

time: 2630 us -> 979 us (0.37)
  waiting for transfers between devices: 1890 us -> 202 us
  blocking collectives: 297 us -> 177 us
  starting transfers between devices: 12.2 us -> 126 us
  matrix products: 181 us -> 225 us
    reduce_scatter x13 -> x0, waiting for transfers between devices: 939 us -> none  [the longest x1 189 us: on_device(): lax.psum_scatter(grad_fc2, 'wide', scatter_dimension=1, tiled=True)]
    unnamed x38 -> x0, waiting for transfers between devices: 840 us -> none
    ppermute x0 -> x97, waiting for transfers between devices: none -> 180 us  [the longest x56 179 us: flip(): return lax.ppermute(operand, 'wide', [(s, s ^ mask) for s in range(size)])]
    all_to_all x3 -> x0, blocking collectives: 122 us -> none  [the longest x1 52.3 us: return_grads(): lax.all_to_all(operand, 'wide', split_axis=0, concat_axis=1, tiled=True)]
    ppermute x0 -> x97, starting transfers between devices: none -> 98 us  [the longest x56 89.6 us: flip(): return lax.ppermute(operand, 'wide', [(s, s ^ mask) for s in range(size)])]
    psum x0 -> x1, blocking collectives: none -> 91.1 us  [on_device(): grad_kv = lax.psum(tp_sum(grad_kv), 'wide').astype(BF)]
    unnamed x2 -> x1, blocking collectives: 125 us -> 39.4 us
    all_gather x8 -> x0, waiting for transfers between devices: 66.1 us -> none  [the longest x4 39.2 us: spread_grads(): return lax.all_gather(operand, 'tp', axis=1, tiled=True)]
  transfers between devices with their start and end apart: 31 -> 102, of which waited for: 26 -> 28; matrix products, arithmetic and copies ran while one was open for 9% -> 45% of each run, Pallas kernels for 0% -> 0%
where the time goes in v1:
time: 979 us; the launch traced here: 969 us
  matrix products  225 us (23%)
  waiting for transfers between devices  202 us (21%)
  blocking collectives  177 us (18%)
  local copies, waits for them, and re-layouts  175 us (18%)
  starting transfers between devices  126 us (13%)
  other arithmetic  59.3 us (6%)
    ppermute x56, waiting for transfers between devices, flip(): return lax.ppermute(operand, 'wide', [(s, s ^ mask) for s in range(size)])  179 us
    psum x1, blocking collectives, on_device(): grad_kv = lax.psum(tp_sum(grad_kv), 'wide').astype(BF)  91.1 us
    ppermute x56, starting transfers between devices, flip(): return lax.ppermute(operand, 'wide', [(s, s ^ mask) for s in range(size)])  89.6 us
    dot_general x30, matrix products, dot_tn(): lax.dot_general(left, right, (((0,), (0,)), ((), ())), preferred_element_...  71.4 us
    dot_general x24, matrix products, dot32(): return jnp.dot(left, right, preferred_element_type=F32)  64.2 us
    dot_general x21, matrix products, dot_nt(): lax.dot_general(left, right, (((1,), (1,)), ((), ())), preferred_element_...  51.4 us
    all_gather x1, blocking collectives, on_device(): keyval = lax.all_gather(keyval_part, 'wide', axis=0, tiled=True)  46.2 us
    unnamed x1, blocking collectives  39.4 us
  transfers between devices with their start and end apart: 102, of which 28 were waited for; matrix products, arithmetic and copies ran while one was open for 45% of the time, Pallas kernels for 0%

profile of v1, /device:TPU:0, one launch (start us, length us, event | category | flops | bytes accessed | tf_op | source)
XLA Modules:
  0.0 969.1 jit_solution(15459642814845626747)
XLA Ops:
  2.8 4.6 fusion.2
  13.3 5.2 copy.198
  25.7 46.2 %all-gather = bf16[16,15,1152]{2,1,0:T(8,128)(2,1)S(1)} all-gather(bf16[1,15,1152]{2,1,0:T(8,128)(2,1)S(1)} %fusion.31), channel_id=1, replica_groups=mesh['wide'=16,'tp'=2] {'wide'}, dimensions={0}, use_global_device_ids=true | all-gather | bytes 587520 | tf_op jit(solution)/shard_map/all_gather | solution.py:225
  73.6 3.7 all-to-all-start.4
  110.6 6.7 all-to-all-start.2
  136.4 7.4 all-to-all-start
  145.4 5.8 fusion.191
  151.2 8.5 all-to-all-done
  199.1 7.1 fusion.23
  206.2 3.5 stack_reshape.16
  209.7 3.5 stack_reshape.18
  213.1 5.7 fusion.190
  218.9 4.3 fusion.192
  232.6 4.4 fusion.193
  237.1 6.8 fusion.30
  243.9 5.0 fusion.68
  294.3 4.8 fusion.78
  323.7 4.3 all-to-all-start.3
  338.8 5.1 fusion.57
  343.9 4.6 fusion.77
  369.5 91.1 %all-reduce.2 = bf16[240,1152]{1,0:T(8,128)(2,1)} all-reduce(f32[240,1152]{1,0:T(8,128)S(1)} %maximum_add_fusion), channel_id=1, replica_groups=mesh['wide'=16,'tp'=2] {'wide'}, use_global_device_ids=true, to_apply=%region_39.40 | all-reduce | flops 276480 | bytes 1658880 | tf_op jit(solution)/shard_map/psum | solution.py:371
  460.6 4.0 fusion.81
  476.3 7.3 collective-permute-done.59
  483.9 4.3 collective-permute-start.60
  496.8 10.6 %collective-permute-done.31 = bf16[256,1152]{1,0:T(8,128)(2,1)S(1)} collective-permute-done((bf16[256,1152]{1,0:T(8,128)(2,1)S(1)}, bf16[256,1152]{1,0:T(8,128)(2,1)S(1)}, u32[]{:S(2)}, u32[]{:S(2)}) %collective-permute-start.31) | collective-permute-done | bytes 589856 | tf_op jit(solution)/shard_map/ppermute | solution.py:110
  514.2 20.0 %collective-permute-done.63 = bf16[72,288]{1,0:T(8,128)(2,1)S(1)} collective-permute-done((bf16[72,288]{1,0:T(8,128)(2,1)S(1)}, bf16[72,288]{1,0:T(8,128)(2,1)S(1)}, u32[]{:S(2)}, u32[]{:S(2)}) %collective-permute-start.63) | collective-permute-done | bytes 41504 | tf_op jit(solution)/shard_map/ppermute | solution.py:110
  534.3 6.4 all-to-all-start.1
  543.7 13.5 %all-to-all-done.1 = bf16[16,2,8,1152]{3,2,1,0:T(8,128)(2,1)S(1)} async-done(((bf16[16,2,8,1152]{3,2,1,0:T(8,128)(2,1)}), bf16[16,2,8,1152]{3,2,1,0:T(8,128)(2,1)S(1)}, u32[]{:S(2)}, u32[]{:S(2)}) %all-to-all-start.1) | async-done | bytes 589856 | tf_op jit(solution)/shard_map/all_to_all | solution.py:247
  569.5 4.0 convolution_add_fusion.5
  573.5 3.9 collective-permute-done.86
  597.2 4.1 copy.203
  614.7 6.4 collective-permute-done.50
  623.9 3.8 collective-permute-done.72
  651.0 3.7 multiply_reduce_fusion
  702.0 11.1 %collective-permute-done.23 = bf16[256,1152]{1,0:T(8,128)(2,1)S(1)} collective-permute-done((bf16[256,1152]{1,0:T(8,128)(2,1)S(1)}, bf16[256,1152]{1,0:T(8,128)(2,1)S(1)}, u32[]{:S(2)}, u32[]{:S(2)}) %collective-permute-start.23) | collective-permute-done | bytes 589856 | tf_op jit(solution)/shard_map/ppermute | solution.py:110
  732.9 39.4 %all-reduce = f32[2,6912]{1,0:T(2,128)S(1)} all-reduce(f32[2,6912]{1,0:T(2,128)} %convolution_dynamic-update-slice_fusion), channel_id=2, replica_groups=mesh['wide'=16,'tp'=2] {'tp','wide'}, use_global_device_ids=true, to_apply=%region_37.38.clone | all-reduce | flops 13824 | bytes 110592
  781.5 4.2 collective-permute-done.40
  787.9 11.0 %collective-permute-done.39 = bf16[2,72,864]{2,1,0:T(8,128)(2,1)S(1)} collective-permute-done((bf16[2,72,864]{2,1,0:T(8,128)(2,1)S(1)}, bf16[2,72,864]{2,1,0:T(8,128)(2,1)S(1)}, u32[]{:S(2)}, u32[]{:S(2)}) %collective-permute-start.39) | collective-permute-done | bytes 248864 | tf_op jit(solution)/shard_map/ppermute | solution.py:110
  804.4 5.4 fusion.4
  813.7 26.5 %collective-permute-done.26 = bf16[4,2,72,288]{3,2,1,0:T(8,128)(2,1)} collective-permute-done((bf16[4,2,72,288]{3,2,1,0:T(8,128)(2,1)}, bf16[4,2,72,288]{3,2,1,0:T(8,128)(2,1)}, u32[]{:S(2)}, u32[]{:S(2)}) %collective-permute-start.26) | collective-permute-done | bytes 331808 | tf_op jit(solution)/shard_map/ppermute | solution.py:110
  844.0 3.5 collective-permute-start.27
  858.1 18.7 %collective-permute-done.30 = bf16[72,288]{1,0:T(8,128)(2,1)S(1)} collective-permute-done((bf16[72,288]{1,0:T(8,128)(2,1)S(1)}, bf16[72,288]{1,0:T(8,128)(2,1)S(1)}, u32[]{:S(2)}, u32[]{:S(2)}) %collective-permute-start.30) | collective-permute-done | bytes 41504 | tf_op jit(solution)/shard_map/ppermute | solution.py:110
  888.3 6.0 collective-permute-done.84
  894.4 18.4 %collective-permute-start.94 = (bf16[2,72,1152]{2,1,0:T(8,128)(2,1)S(1)}, bf16[2,72,1152]{2,1,0:T(8,128)(2,1)S(1)}, u32[]{:S(2)}, u32[]{:S(2)}) collective-permute-start(bf16[2,72,1152]{2,1,0:T(8,128)(2,1)S(1)} %get-tuple-element.56), channel_id=1, source_target_pairs={{0,16},{2,18},{4,20},{6,22},{8,24},{10,26},{12,28},{14,30},{16,0},... | collective-permute-start | bytes 995336 | tf_op jit(solution)/shard_map/ppermute | solution.py:110
  912.8 11.3 %collective-permute-done.83 = bf16[2,72,1152]{2,1,0:T(8,128)(2,1)S(1)} collective-permute-done((bf16[2,72,1152]{2,1,0:T(8,128)(2,1)S(1)}, bf16[2,72,1152]{2,1,0:T(8,128)(2,1)S(1)}, u32[]{:S(2)}, u32[]{:S(2)}) %collective-permute-start.83) | collective-permute-done | bytes 331808 | tf_op jit(solution)/shard_map/ppermute | solution.py:110
  925.8 10.6 %collective-permute-done.94 = bf16[2,72,1152]{2,1,0:T(8,128)(2,1)S(1)} collective-permute-done((bf16[2,72,1152]{2,1,0:T(8,128)(2,1)S(1)}, bf16[2,72,1152]{2,1,0:T(8,128)(2,1)S(1)}, u32[]{:S(2)}, u32[]{:S(2)}) %collective-permute-start.94) | collective-permute-done | bytes 331808 | tf_op jit(solution)/shard_map/ppermute | solution.py:110
  947.1 5.2 collective-permute-done.21
  952.4 9.1 collective-permute-done.20
  (869 shorter events, 454.2 us)
Async XLA Ops:
  0.7 76.7 %collective-permute-start.1 = (bf16[2,128,1152]{2,1,0:T(8,128)(2,1)}, bf16[2,128,1152]{2,1,0:T(8,128)(2,1)S(1)}, u32[]{:S(2)}, u32[]{:S(2)}) collective-permute-start(bf16[2,128,1152]{2,1,0:T(8,128)(2,1)} %param.18), channel_id=1, source_target_pairs={{0,1},{1,0},{2,3},{3,2},{4,5},{5,4},{6,7},{7,6},{8,9},{9,8},{10,11... | collective-permute-start | bytes 1769480 | tf_op jit(solution)/shard_map/ppermute | solution.py:83
  7.5 163.1 %collective-permute-start.3 = (bf16[3,576,1152]{2,1,0:T(8,128)(2,1)}, bf16[3,576,1152]{2,1,0:T(8,128)(2,1)}, u32[]{:S(2)}, u32[]{:S(2)}) collective-permute-start(bf16[3,576,1152]{2,1,0:T(8,128)(2,1)} %bitcast.21), channel_id=1, source_target_pairs={{0,1},{1,0},{2,3},{3,2},{4,5},{5,4},{6,7},{7,6},{8,9},{9,8},{10,11... | collective-permute-start | bytes 11943944 | tf_op jit(solution)/shard_map/ppermute | solution.py:83
  7.9 170.4 %collective-permute-start.4 = (bf16[576,1152]{1,0:T(8,128)(2,1)}, bf16[576,1152]{1,0:T(8,128)(2,1)}, u32[]{:S(2)}, u32[]{:S(2)}) collective-permute-start(bf16[576,1152]{1,0:T(8,128)(2,1)} %param.30), channel_id=1, source_target_pairs={{0,1},{1,0},{2,3},{3,2},{4,5},{5,4},{6,7},{7,6},{8,9},{9,8},{10,11... | collective-permute-start | bytes 3981320 | tf_op jit(solution)/shard_map/ppermute | solution.py:83
  20.0 166.7 %collective-permute-start.6 = (bf16[576,1152]{1,0:T(8,128)(2,1)}, bf16[576,1152]{1,0:T(8,128)(2,1)}, u32[]{:S(2)}, u32[]{:S(2)}) collective-permute-start(bf16[576,1152]{1,0:T(8,128)(2,1)} %bitcast.935), channel_id=1, source_target_pairs={{0,1},{1,0},{2,3},{3,2},{4,5},{5,4},{6,7},{7,6},{8,9},{9,8},{10,11... | collective-permute-start | bytes 3981320 | tf_op jit(solution)/shard_map/ppermute | solution.py:83
  72.9 50.8 %collective-permute-start.7 = (bf16[240,1152]{1,0:T(8,128)(2,1)}, bf16[240,1152]{1,0:T(8,128)(2,1)}, u32[]{:S(2)}, u32[]{:S(2)}) collective-permute-start(bf16[240,1152]{1,0:T(8,128)(2,1)} %reshape.1186), channel_id=1, source_target_pairs={{0,1},{1,0},{2,3},{3,2},{4,5},{5,4},{6,7},{7,6},{8,9},{9,8},{10,11... | collective-permute-start | bytes 1658888 | tf_op jit(solution)/shard_map/ppermute | solution.py:83
  73.6 36.3 %all-to-all-start.4 = ((bf16[16,15,328]{2,1,0:T(8,128)(2,1)}), bf16[16,15,328]{2,1,0:T(8,128)(2,1)S(1)}, u32[]{:S(2)}, u32[]{:S(2)}) async-start(bf16[16,15,328]{2,1,0:T(8,128)(2,1)} %maximum_bitcast_fusion), calls=%async_computation.4 | async-start | bytes 393216 | tf_op jit(solution)/shard_map/all_to_all | solution.py:236
  109.4 23.9 %collective-permute-start.2 = (bf16[2,128,1152]{2,1,0:T(8,128)(2,1)}, bf16[2,128,1152]{2,1,0:T(8,128)(2,1)}, u32[]{:S(2)}, u32[]{:S(2)}) collective-permute-start(bf16[2,128,1152]{2,1,0:T(8,128)(2,1)} %bitcast.16), channel_id=1, source_target_pairs={{0,1},{1,0},{2,3},{3,2},{4,5},{5,4},{6,7},{7,6},{8,9},{9,8},{10,11... | collective-permute-start | bytes 1769480 | tf_op jit(solution)/shard_map/ppermute | solution.py:88
  110.6 25.8 %all-to-all-start.2 = ((bf16[16,2,8,1152]{3,2,1,0:T(8,128)(2,1)}), bf16[16,2,8,1152]{3,2,1,0:T(8,128)(2,1)S(1)}, u32[]{:S(2)}, u32[]{:S(2)}) async-start(bf16[16,2,8,1152]{3,2,1,0:T(8,128)(2,1)} %copy_bitcast_fusion.3), calls=%async_computation.2 | async-start | bytes 1179648 | tf_op jit(solution)/shard_map/all_to_all | solution.py:242
  123.6 69.9 %collective-permute-start.8 = (bf16[576,1152]{1,0:T(8,128)(2,1)}, bf16[576,1152]{1,0:T(8,128)(2,1)}, u32[]{:S(2)}, u32[]{:S(2)}) collective-permute-start(bf16[576,1152]{1,0:T(8,128)(2,1)} %param.33), channel_id=1, source_target_pairs={{0,1},{1,0},{2,3},{3,2},{4,5},{5,4},{6,7},{7,6},{8,9},{9,8},{10,11... | collective-permute-start | bytes 3981320 | tf_op jit(solution)/shard_map/ppermute | solution.py:83
  133.3 99.0 %collective-permute-start.10 = (bf16[2304,1152]{1,0:T(8,128)(2,1)}, bf16[2304,1152]{1,0:T(8,128)(2,1)}, u32[]{:S(2)}, u32[]{:S(2)}) collective-permute-start(bf16[2304,1152]{1,0:T(8,128)(2,1)} %param.35), channel_id=1, source_target_pairs={{0,1},{1,0},{2,3},{3,2},{4,5},{5,4},{6,7},{7,6},{8,9},{9,8},{10,11... | collective-permute-start | bytes 15925256 | tf_op jit(solution)/shard_map/ppermute | solution.py:83
  136.4 23.3 %all-to-all-start = ((bf16[16,2,8,1152]{3,2,1,0:T(8,128)(2,1)}), bf16[16,2,8,1152]{3,2,1,0:T(8,128)(2,1)S(1)}, u32[]{:S(2)}, u32[]{:S(2)}) async-start(bf16[16,2,8,1152]{3,2,1,0:T(8,128)(2,1)} %copy_bitcast_fusion.5), calls=%async_computation | async-start | bytes 1179648 | tf_op jit(solution)/shard_map/all_to_all | solution.py:242
  170.6 66.4 %collective-permute-start.9 = (bf16[1152,2304]{1,0:T(8,128)(2,1)}, bf16[1152,2304]{1,0:T(8,128)(2,1)}, u32[]{:S(2)}, u32[]{:S(2)}) collective-permute-start(bf16[1152,2304]{1,0:T(8,128)(2,1)} %param.34), channel_id=1, source_target_pairs={{0,1},{1,0},{2,3},{3,2},{4,5},{5,4},{6,7},{7,6},{8,9},{9,8},{10,11... | collective-permute-start | bytes 15925256 | tf_op jit(solution)/shard_map/ppermute | solution.py:83
  182.5 49.6 %collective-permute-start.53 = (bf16[256,1152]{1,0:T(8,128)(2,1)}, bf16[256,1152]{1,0:T(8,128)(2,1)}, u32[]{:S(2)}, u32[]{:S(2)}) collective-permute-start(bf16[256,1152]{1,0:T(8,128)(2,1)} %fusion.69), channel_id=1, source_target_pairs={{0,2},{2,0},{4,6},{6,4},{8,10},{10,8},{12,14},{14,12},{16,18},{18,... | collective-permute-start | bytes 1769480 | tf_op jit(solution)/shard_map/ppermute | solution.py:110
  186.6 40.8 %collective-permute-start.43 = (bf16[2,256,1,288]{1,3,0,2:T(8,128)(2,1)}, bf16[2,256,1,288]{1,3,0,2:T(8,128)(2,1)}, u32[]{:S(2)}, u32[]{:S(2)}) collective-permute-start(bf16[2,256,1,288]{1,3,0,2:T(8,128)(2,1)} %get-tuple-element.84), channel_id=1, source_target_pairs={{0,4},{2,6},{4,0},{6,2},{8,12},{10,14},{12,8},{14,10},{16,20},{18,... | collective-permute-start | bytes 884744 | tf_op jit(solution)/shard_map/ppermute | solution.py:110
  196.8 32.2 %collective-permute-start.65 = (bf16[2,256,1,288]{1,3,0,2:T(8,128)(2,1)}, bf16[2,256,1,288]{1,3,0,2:T(8,128)(2,1)}, u32[]{:S(2)}, u32[]{:S(2)}) collective-permute-start(bf16[2,256,1,288]{1,3,0,2:T(8,128)(2,1)} %get-tuple-element.80), channel_id=1, source_target_pairs={{0,4},{2,6},{4,0},{6,2},{8,12},{10,14},{12,8},{14,10},{16,20},{18,... | collective-permute-start | bytes 884744 | tf_op jit(solution)/shard_map/ppermute | solution.py:110
  227.4 131.0 %collective-permute-start.55 = (bf16[256,1152]{1,0:T(8,128)(2,1)}, bf16[256,1152]{1,0:T(8,128)(2,1)}, u32[]{:S(2)}, u32[]{:S(2)}) collective-permute-start(bf16[256,1152]{1,0:T(8,128)(2,1)} %fusion.69), channel_id=1, source_target_pairs={{0,1},{1,0},{2,3},{3,2},{4,5},{5,4},{6,7},{7,6},{8,9},{9,8},{10,11... | collective-permute-start | bytes 1769480 | tf_op jit(solution)/shard_map/ppermute | solution.py:88
  229.0 339.9 %collective-permute-start.75 = (bf16[256,1152]{1,0:T(8,128)(2,1)}, bf16[256,1152]{1,0:T(8,128)(2,1)}, u32[]{:S(2)}, u32[]{:S(2)}) collective-permute-start(bf16[256,1152]{1,0:T(8,128)(2,1)} %fusion.46), channel_id=1, source_target_pairs={{0,2},{2,0},{4,6},{6,4},{8,10},{10,8},{12,14},{14,12},{16,18},{18,... | collective-permute-start | bytes 1769480 | tf_op jit(solution)/shard_map/ppermute | solution.py:110
  232.1 239.0 %collective-permute-start.45 = (bf16[256,288]{0,1:T(8,128)(2,1)}, bf16[256,288]{0,1:T(8,128)(2,1)}, u32[]{:S(2)}, u32[]{:S(2)}) collective-permute-start(bf16[256,288]{0,1:T(8,128)(2,1)} %slice_bitcast_fusion.47), channel_id=1, source_target_pairs={{0,1},{1,0},{2,3},{3,2},{4,5},{5,4},{6,7},{7,6},{8,9},{9,8},{10,11... | collective-permute-start | bytes 442376 | tf_op jit(solution)/shard_map/ppermute | solution.py:88
  232.3 128.2 %collective-permute-start.57 = (bf16[256,1152]{1,0:T(8,128)(2,1)}, bf16[256,1152]{1,0:T(8,128)(2,1)}, u32[]{:S(2)}, u32[]{:S(2)}) collective-permute-start(bf16[256,1152]{1,0:T(8,128)(2,1)} %collective-permute-done.53), channel_id=1, source_target_pairs={{0,1},{1,0},{2,3},{3,2},{4,5},{5,4},{6,7},{7,6},{8,9},{9,8},{10,11... | collective-permute-start | bytes 1769480 | tf_op jit(solution)/shard_map/ppermute | solution.py:88
  323.7 210.6 %all-to-all-start.3 = ((bf16[16,2,8,1152]{3,2,1,0:T(8,128)(2,1)}), bf16[16,2,8,1152]{3,2,1,0:T(8,128)(2,1)S(1)}, u32[]{:S(2)}, u32[]{:S(2)}) async-start(bf16[16,2,8,1152]{3,2,1,0:T(8,128)(2,1)} %bitcast.920), calls=%async_computation.3 | async-start | bytes 1179648 | tf_op jit(solution)/shard_map/all_to_all | solution.py:247
  360.5 113.1 %collective-permute-start.67 = (bf16[256,288]{0,1:T(8,128)(2,1)}, bf16[256,288]{0,1:T(8,128)(2,1)}, u32[]{:S(2)}, u32[]{:S(2)}) collective-permute-start(bf16[256,288]{0,1:T(8,128)(2,1)} %slice_bitcast_fusion.35), channel_id=1, source_target_pairs={{0,1},{1,0},{2,3},{3,2},{4,5},{5,4},{6,7},{7,6},{8,9},{9,8},{10,11... | collective-permute-start | bytes 442376 | tf_op jit(solution)/shard_map/ppermute | solution.py:88
  361.0 106.0 %collective-permute-start.42 = (bf16[256,1152]{1,0:T(8,128)(2,1)}, bf16[256,1152]{1,0:T(8,128)(2,1)}, u32[]{:S(2)}, u32[]{:S(2)}) collective-permute-start(bf16[256,1152]{1,0:T(8,128)(2,1)} %get-tuple-element.42), channel_id=1, source_target_pairs={{0,4},{2,6},{4,0},{6,2},{8,12},{10,14},{12,8},{14,10},{16,20},{18,... | collective-permute-start | bytes 1769480 | tf_op jit(solution)/shard_map/ppermute | solution.py:110
  367.3 101.8 %collective-permute-start.64 = (bf16[256,1152]{1,0:T(8,128)(2,1)}, bf16[256,1152]{1,0:T(8,128)(2,1)}, u32[]{:S(2)}, u32[]{:S(2)}) collective-permute-start(bf16[256,1152]{1,0:T(8,128)(2,1)} %copy-done.85), channel_id=1, source_target_pairs={{0,4},{2,6},{4,0},{6,2},{8,12},{10,14},{12,8},{14,10},{16,20},{18,... | collective-permute-start | bytes 1769480 | tf_op jit(solution)/shard_map/ppermute | solution.py:110
  471.1 24.3 %collective-permute-start.32 = (bf16[2,256,3,288]{1,3,2,0:T(8,128)(2,1)S(1)}, bf16[2,256,3,288]{1,3,2,0:T(8,128)(2,1)S(1)}, u32[]{:S(2)}, u32[]{:S(2)}) collective-permute-start(bf16[2,256,3,288]{1,3,2,0:T(8,128)(2,1)S(1)} %copy-done.122), channel_id=1, source_target_pairs={{0,2},{2,0},{4,6},{6,4},{8,10},{10,8},{12,14},{14,12},{16,18},{18,... | collective-permute-start | bytes 2654216 | tf_op jit(solution)/shard_map/ppermute | solution.py:110
  491.7 51.8 %collective-permute-start.47 = (bf16[256,288]{0,1:T(8,128)(2,1)}, bf16[256,288]{0,1:T(8,128)(2,1)S(1)}, u32[]{:S(2)}, u32[]{:S(2)}) collective-permute-start(bf16[256,288]{0,1:T(8,128)(2,1)} %slice_bitcast_fusion.46), channel_id=1, source_target_pairs={{0,1},{1,0},{2,3},{3,2},{4,5},{5,4},{6,7},{7,6},{8,9},{9,8},{10,11... | collective-permute-start | bytes 442376 | tf_op jit(solution)/shard_map/ppermute | solution.py:88
  507.4 61.5 %collective-permute-start.76 = (bf16[2,256,1,1152]{3,1,0,2:T(8,128)(2,1)}, bf16[2,256,1,1152]{3,1,0,2:T(8,128)(2,1)}, u32[]{:S(2)}, u32[]{:S(2)}) collective-permute-start(bf16[2,256,1,1152]{3,1,0,2:T(8,128)(2,1)} %dynamic-slice_bitcast_fusion.3), channel_id=1, source_target_pairs={{0,2},{2,0},{4,6},{6,4},{8,10},{10,8},{12,14},{14,12},{16,18},{18,... | collective-permute-start | bytes 3538952 | tf_op jit(solution)/shard_map/ppermute | solution.py:110
  509.9 67.5 %collective-permute-start.87 = (bf16[2,256,1,1152]{3,1,0,2:T(8,128)(2,1)}, bf16[2,256,1,1152]{3,1,0,2:T(8,128)(2,1)}, u32[]{:S(2)}, u32[]{:S(2)}) collective-permute-start(bf16[2,256,1,1152]{3,1,0,2:T(8,128)(2,1)} %dynamic-slice_bitcast_fusion.2), channel_id=1, source_target_pairs={{0,4},{2,6},{4,0},{6,2},{8,12},{10,14},{12,8},{14,10},{16,20},{18,... | collective-permute-start | bytes 3538952 | tf_op jit(solution)/shard_map/ppermute | solution.py:110
  510.5 23.8 %collective-permute-start.63 = (bf16[72,288]{1,0:T(8,128)(2,1)S(1)}, bf16[72,288]{1,0:T(8,128)(2,1)S(1)}, u32[]{:S(2)}, u32[]{:S(2)}) collective-permute-start(bf16[72,288]{1,0:T(8,128)(2,1)S(1)} %fusion.135), channel_id=1, source_target_pairs={{0,2},{2,0},{4,6},{6,4},{8,10},{10,8},{12,14},{14,12},{16,18},{18,... | collective-permute-start | bytes 124424 | tf_op jit(solution)/shard_map/ppermute | solution.py:110
  534.3 24.8 %collective-permute-start.46 = (bf16[256,1152]{1,0:T(8,128)(2,1)}, bf16[256,1152]{1,0:T(8,128)(2,1)}, u32[]{:S(2)}, u32[]{:S(2)}) collective-permute-start(bf16[256,1152]{1,0:T(8,128)(2,1)} %collective-permute-done.42), channel_id=1, source_target_pairs={{0,1},{1,0},{2,3},{3,2},{4,5},{5,4},{6,7},{7,6},{8,9},{9,8},{10,11... | collective-permute-start | bytes 1769480 | tf_op jit(solution)/shard_map/ppermute | solution.py:88
  561.0 128.8 %collective-permute-start.15 = (bf16[256,1152]{1,0:T(8,128)(2,1)}, bf16[256,1152]{1,0:T(8,128)(2,1)}, u32[]{:S(2)}, u32[]{:S(2)}) collective-permute-start(bf16[256,1152]{1,0:T(8,128)(2,1)} %bitcast.152), channel_id=1, source_target_pairs={{0,2},{2,0},{4,6},{6,4},{8,10},{10,8},{12,14},{14,12},{16,18},{18,... | collective-permute-start | bytes 1769480 | tf_op jit(solution)/shard_map/ppermute | solution.py:110
  583.0 112.0 %collective-permute-start.90 = (bf16[256,1152]{1,0:T(8,128)(2,1)}, bf16[256,1152]{1,0:T(8,128)(2,1)}, u32[]{:S(2)}, u32[]{:S(2)}) collective-permute-start(bf16[256,1152]{1,0:T(8,128)(2,1)} %collective-permute-done.86), channel_id=1, source_target_pairs={{0,1},{1,0},{2,3},{3,2},{4,5},{5,4},{6,7},{7,6},{8,9},{9,8},{10,11... | collective-permute-start | bytes 1769480 | tf_op jit(solution)/shard_map/ppermute | solution.py:88
  623.8 68.6 %collective-permute-start.79 = (bf16[256,1152]{1,0:T(8,128)(2,1)}, bf16[256,1152]{1,0:T(8,128)(2,1)}, u32[]{:S(2)}, u32[]{:S(2)}) collective-permute-start(bf16[256,1152]{1,0:T(8,128)(2,1)} %collective-permute-done.75), channel_id=1, source_target_pairs={{0,1},{1,0},{2,3},{3,2},{4,5},{5,4},{6,7},{7,6},{8,9},{9,8},{10,11... | collective-permute-start | bytes 1769480 | tf_op jit(solution)/shard_map/ppermute | solution.py:88
  636.8 55.6 %collective-permute-start.80 = (bf16[256,1152]{1,0:T(8,128)(2,1)}, bf16[256,1152]{1,0:T(8,128)(2,1)}, u32[]{:S(2)}, u32[]{:S(2)}) collective-permute-start(bf16[256,1152]{1,0:T(8,128)(2,1)} %slice_bitcast_fusion.31), channel_id=1, source_target_pairs={{0,1},{1,0},{2,3},{3,2},{4,5},{5,4},{6,7},{7,6},{8,9},{9,8},{10,11... | collective-permute-start | bytes 1769480 | tf_op jit(solution)/shard_map/ppermute | solution.py:88
  638.7 58.2 %collective-permute-start.91 = (bf16[256,1152]{1,0:T(8,128)(2,1)}, bf16[256,1152]{1,0:T(8,128)(2,1)}, u32[]{:S(2)}, u32[]{:S(2)}) collective-permute-start(bf16[256,1152]{1,0:T(8,128)(2,1)} %slice_bitcast_fusion.28), channel_id=1, source_target_pairs={{0,1},{1,0},{2,3},{3,2},{4,5},{5,4},{6,7},{7,6},{8,9},{9,8},{10,11... | collective-permute-start | bytes 1769480 | tf_op jit(solution)/shard_map/ppermute | solution.py:88
  690.6 25.0 %collective-permute-start.25 = (bf16[512,1,288]{0,2,1:T(8,128)(2,1)S(1)}, bf16[512,1,288]{0,2,1:T(8,128)(2,1)S(1)}, u32[]{:S(2)}, u32[]{:S(2)}) collective-permute-start(bf16[512,1,288]{0,2,1:T(8,128)(2,1)S(1)} %copy-done.143), channel_id=1, source_target_pairs={{0,4},{2,6},{4,0},{6,2},{8,12},{10,14},{12,8},{14,10},{16,20},{18,... | collective-permute-start | bytes 884744 | tf_op jit(solution)/shard_map/ppermute | solution.py:110
  692.4 109.9 %collective-permute-start.16 = (bf16[256,1152]{1,0:T(8,128)(2,1)}, bf16[256,1152]{1,0:T(8,128)(2,1)}, u32[]{:S(2)}, u32[]{:S(2)}) collective-permute-start(bf16[256,1152]{1,0:T(8,128)(2,1)} %collective-permute-done.15), channel_id=1, source_target_pairs={{0,1},{1,0},{2,3},{3,2},{4,5},{5,4},{6,7},{7,6},{8,9},{9,8},{10,11... | collective-permute-start | bytes 1769480 | tf_op jit(solution)/shard_map/ppermute | solution.py:83
  695.0 78.0 %collective-permute-start.37 = (bf16[4,2,72,864]{3,2,1,0:T(8,128)(2,1)}, bf16[4,2,72,864]{3,2,1,0:T(8,128)(2,1)}, u32[]{:S(2)}, u32[]{:S(2)}) collective-permute-start(bf16[4,2,72,864]{3,2,1,0:T(8,128)(2,1)} %dynamic-slice_bitcast_fusion.4), channel_id=1, source_target_pairs={{0,4},{2,6},{4,0},{6,2},{8,12},{10,14},{12,8},{14,10},{16,20},{18,... | collective-permute-start | bytes 2985992 | tf_op jit(solution)/shard_map/ppermute | solution.py:110
  713.1 91.3 %collective-permute-start.17 = (bf16[512,3,288]{0,2,1:T(8,128)(2,1)}, bf16[512,3,288]{0,2,1:T(8,128)(2,1)}, u32[]{:S(2)}, u32[]{:S(2)}) collective-permute-start(bf16[512,3,288]{0,2,1:T(8,128)(2,1)} %get-tuple-element.52), channel_id=1, source_target_pairs={{0,2},{2,0},{4,6},{6,4},{8,10},{10,8},{12,14},{14,12},{16,18},{18,... | collective-permute-start | bytes 2654216 | tf_op jit(solution)/shard_map/ppermute | solution.py:110
  777.2 23.9 %collective-permute-start.38 = (bf16[2,72,864]{2,1,0:T(8,128)(2,1)S(1)}, bf16[2,72,864]{2,1,0:T(8,128)(2,1)S(1)}, u32[]{:S(2)}, u32[]{:S(2)}) collective-permute-start(bf16[2,72,864]{2,1,0:T(8,128)(2,1)S(1)} %get-tuple-element.62), channel_id=1, source_target_pairs={{0,8},{2,10},{4,12},{6,14},{8,0},{10,2},{12,4},{14,6},{16,24},{18,... | collective-permute-start | bytes 746504 | tf_op jit(solution)/shard_map/ppermute | solution.py:110
  785.7 93.8 %collective-permute-start.81 = (bf16[4,2,72,1152]{3,2,1,0:T(8,128)(2,1)}, bf16[4,2,72,1152]{3,2,1,0:T(8,128)(2,1)}, u32[]{:S(2)}, u32[]{:S(2)}) collective-permute-start(bf16[4,2,72,1152]{3,2,1,0:T(8,128)(2,1)} %dynamic-slice_bitcast_fusion.1), channel_id=1, source_target_pairs={{0,4},{2,6},{4,0},{6,2},{8,12},{10,14},{12,8},{14,10},{16,20},{18,... | collective-permute-start | bytes 3981320 | tf_op jit(solution)/shard_map/ppermute | solution.py:110
  798.9 87.3 %collective-permute-start.92 = (bf16[4,2,72,1152]{3,2,1,0:T(8,128)(2,1)}, bf16[4,2,72,1152]{3,2,1,0:T(8,128)(2,1)}, u32[]{:S(2)}, u32[]{:S(2)}) collective-permute-start(bf16[4,2,72,1152]{3,2,1,0:T(8,128)(2,1)} %dynamic-slice_bitcast_fusion), channel_id=1, source_target_pairs={{0,2},{2,0},{4,6},{6,4},{8,10},{10,8},{12,14},{14,12},{16,18},{18,... | collective-permute-start | bytes 3981320 | tf_op jit(solution)/shard_map/ppermute | solution.py:110
  801.1 39.1 %collective-permute-start.26 = (bf16[4,2,72,288]{3,2,1,0:T(8,128)(2,1)}, bf16[4,2,72,288]{3,2,1,0:T(8,128)(2,1)}, u32[]{:S(2)}, u32[]{:S(2)}) collective-permute-start(bf16[4,2,72,288]{3,2,1,0:T(8,128)(2,1)} %dynamic-slice_bitcast_fusion.17), channel_id=1, source_target_pairs={{0,2},{2,0},{4,6},{6,4},{8,10},{10,8},{12,14},{14,12},{16,18},{18,... | collective-permute-start | bytes 995336 | tf_op jit(solution)/shard_map/ppermute | solution.py:110
  802.3 41.6 %collective-permute-start.41 = (bf16[72,864]{1,0:T(8,128)(2,1)S(1)}, bf16[72,864]{1,0:T(8,128)(2,1)}, u32[]{:S(2)}, u32[]{:S(2)}) collective-permute-start(bf16[72,864]{1,0:T(8,128)(2,1)S(1)} %fusion.130), channel_id=1, source_target_pairs={{0,2},{2,0},{4,6},{6,4},{8,10},{10,8},{12,14},{14,12},{16,18},{18,... | collective-permute-start | bytes 373256 | tf_op jit(solution)/shard_map/ppermute | solution.py:110
  854.9 84.9 %collective-permute-start.18 = (bf16[4,2,72,864]{3,2,1,0:T(8,128)(2,1)}, bf16[4,2,72,864]{3,2,1,0:T(8,128)(2,1)}, u32[]{:S(2)}, u32[]{:S(2)}) collective-permute-start(bf16[4,2,72,864]{3,2,1,0:T(8,128)(2,1)} %dynamic-slice_bitcast_fusion.5), channel_id=1, source_target_pairs={{0,4},{2,6},{4,0},{6,2},{8,12},{10,14},{12,8},{14,10},{16,20},{18,... | collective-permute-start | bytes 2985992 | tf_op jit(solution)/shard_map/ppermute | solution.py:110
  882.1 42.0 %collective-permute-start.83 = (bf16[2,72,1152]{2,1,0:T(8,128)(2,1)S(1)}, bf16[2,72,1152]{2,1,0:T(8,128)(2,1)S(1)}, u32[]{:S(2)}, u32[]{:S(2)}) collective-permute-start(bf16[2,72,1152]{2,1,0:T(8,128)(2,1)S(1)} %get-tuple-element.59), channel_id=1, source_target_pairs={{0,16},{2,18},{4,20},{6,22},{8,24},{10,26},{12,28},{14,30},{16,0},... | collective-permute-start | bytes 995336 | tf_op jit(solution)/shard_map/ppermute | solution.py:110
  883.6 40.5 %collective-permute-start.82 = (bf16[2,72,1152]{2,1,0:T(8,128)(2,1)S(1)}, bf16[2,72,1152]{2,1,0:T(8,128)(2,1)S(1)}, u32[]{:S(2)}, u32[]{:S(2)}) collective-permute-start(bf16[2,72,1152]{2,1,0:T(8,128)(2,1)S(1)} %get-tuple-element.57), channel_id=1, source_target_pairs={{0,8},{2,10},{4,12},{6,14},{8,0},{10,2},{12,4},{14,6},{16,24},{18,... | collective-permute-start | bytes 995336 | tf_op jit(solution)/shard_map/ppermute | solution.py:110
  888.0 37.8 %collective-permute-start.95 = (bf16[2,72,1152]{2,1,0:T(8,128)(2,1)S(1)}, bf16[2,72,1152]{2,1,0:T(8,128)(2,1)S(1)}, u32[]{:S(2)}, u32[]{:S(2)}) collective-permute-start(bf16[2,72,1152]{2,1,0:T(8,128)(2,1)S(1)} %get-tuple-element.55), channel_id=1, source_target_pairs={{0,24},{2,26},{4,28},{6,30},{8,16},{10,18},{12,20},{14,22},{16,8},... | collective-permute-start | bytes 995336 | tf_op jit(solution)/shard_map/ppermute | solution.py:110
  894.4 42.0 %collective-permute-start.94 = (bf16[2,72,1152]{2,1,0:T(8,128)(2,1)S(1)}, bf16[2,72,1152]{2,1,0:T(8,128)(2,1)S(1)}, u32[]{:S(2)}, u32[]{:S(2)}) collective-permute-start(bf16[2,72,1152]{2,1,0:T(8,128)(2,1)S(1)} %get-tuple-element.56), channel_id=1, source_target_pairs={{0,16},{2,18},{4,20},{6,22},{8,24},{10,26},{12,28},{14,30},{16,0},... | collective-permute-start | bytes 995336 | tf_op jit(solution)/shard_map/ppermute | solution.py:110
  (223 other events, 1889.4 us)
